TPU v7x, 512 devices: a whole 4x4x16 slice. The times are simulated.
512 devices in a mesh: dp: 32 (over x, y, core), vocab: 16 (over z).
Axes of the slice: x: 4, y: 4, z: 16, core: 2. Of those that a mesh axis runs over, the one named last changes fastest.
Arguments:
- query_hidden: bfloat16 [64, 32, 4096], P('dp'), may hold values from -6 to 6
- passage_hidden: bfloat16 [64, 96, 4096], P('dp'), may hold values from -6 to 6
- query_logits: float32 [64, 32, 16384], P('dp', None, 'vocab'), may hold values from -12 to 6
- passage_logits: float32 [64, 96, 16384], P('dp', None, 'vocab'), may hold values from -12 to 6
- head_weight: bfloat16 [16384, 4096], P('vocab', 'dp'), may hold values from -0.1875 to 0.1875
- query_mask: int32 [64, 32], P('dp'), may hold values from 0 to 1, as said below
- passage_mask: int32 [64, 96], P('dp'), may hold values from 0 to 1, as said below
- positive: int32 [64], replicated, may hold values from 0 to 63, as said below
- score_scale: float32 [1], replicated, may hold values from 256 to 768
Outputs:
- grad_query_hidden: bfloat16 [64, 32, 4096], P('dp', None, 'vocab')
- grad_passage_hidden: bfloat16 [64, 96, 4096], P('dp', None, 'vocab')
- grad_weight: float32 [16384, 4096], P('vocab', 'dp')
Inputs may be any that keep to these rules, and one draw needn't show every extreme that they name: `query_mask`: each row is 1 on its first positions, at least 8 of them, and 0 after them. `passage_mask`: each row is 1 on its first positions, at least 24 of them, and 0 after them. The positive passage of query i is one of the 2 passages of its own group, from 2 * (i // 2) to 2 * (i // 2) + 1.
All inputs are finite; a program needn't handle non-finite values.
Results may differ from a plain program's by a relative error of at most 0.023.
Values may be sent and summed in bfloat16 or wider, within the bound.
A program may use at most 64 MiB of HBM per device.

v0:
```python
import jax
import jax.numpy as jnp
from jax import lax
from jax.sharding import PartitionSpec as P

loss_scale = 256.0
query_weight = 3.0
passage_weight = 1.0
highest = lax.Precision.HIGHEST


def pooling(logits, padding):
    masked = jnp.where(padding[:, :, None] > 0, logits, -jnp.inf)
    return (jnp.max(masked, axis=1), jnp.argmax(masked, axis=1))


def activate(pooled):
    return jnp.log1p(jnp.maximum(pooled, 0.0))


def slopes(pooled):
    return jnp.where(pooled > 0.0, 1.0 / (1.0 + jnp.maximum(pooled, 0.0)), 0.0)


def softmax_excess(scores, positive):
    largest = jnp.max(scores, axis=1, keepdims=True)
    weights = jnp.exp(scores - largest)
    target = (jnp.arange(scores.shape[1], dtype=jnp.int32)[None, :] == positive[:, None]).astype(
        jnp.float32
    )
    return weights / jnp.sum(weights, axis=1, keepdims=True) - target


def spread(push_rows, spot_rows, positions):
    return jnp.where(
        positions[None, :, None] == spot_rows[:, None, :],
        push_rows[:, None, :],
        jnp.zeros((), jnp.bfloat16),
    )


def on_device(
    query_hidden,
    passage_hidden,
    query_logits,
    passage_logits,
    head_weight,
    query_mask,
    passage_mask,
    positive,
    score_scale,
):
    query_count = query_logits.shape[0]
    query_length = query_logits.shape[1]
    vocab_local = query_logits.shape[2]
    passage_count = passage_logits.shape[0]
    passage_length = passage_logits.shape[1]
    groups = lax.axis_size("dp")
    query_pool, query_where = pooling(query_logits, query_mask)
    passage_pool, passage_where = pooling(passage_logits, passage_mask)
    query_columns, passage_columns = (
        lax.all_to_all(query_hidden, "dp", split_axis=2, concat_axis=0, tiled=True),
        lax.all_to_all(passage_hidden, "dp", split_axis=2, concat_axis=0, tiled=True),
    )
    all_query, all_passage, query_spots, passage_spots = (
        lax.all_gather(query_pool, "dp", axis=0, tiled=True),
        lax.all_gather(passage_pool, "dp", axis=0, tiled=True),
        lax.all_gather(query_where, "dp", axis=0, tiled=True),
        lax.all_gather(passage_where, "dp", axis=0, tiled=True),
    )
    query_rep = activate(all_query)
    passage_rep = activate(all_passage)
    factor = score_scale[0] / (vocab_local * lax.axis_size("vocab"))
    partial_value = jnp.dot(query_rep, passage_rep.T, precision=highest)
    scores = lax.psum(partial_value, "vocab") * factor
    excess = softmax_excess(scores, positive)
    query_total = query_rep.shape[0]
    passage_total = passage_rep.shape[0]
    query_mean = jnp.sum(query_rep, axis=0) / query_total
    passage_mean = jnp.sum(passage_rep, axis=0) / passage_total
    query_grad = loss_scale * (
        factor * jnp.dot(excess, passage_rep, precision=highest)
        + 2.0 * query_weight / query_total * query_mean[None, :]
    )
    passage_grad = loss_scale * (
        factor * jnp.dot(excess.T, query_rep, precision=highest)
        + 2.0 * passage_weight / passage_total * passage_mean[None, :]
    )
    query_push = (query_grad * slopes(all_query)).astype(jnp.bfloat16)
    passage_push = (passage_grad * slopes(all_passage)).astype(jnp.bfloat16)
    blocks = groups // 2
    query_items = (
        query_push.reshape(blocks, 2 * query_count, vocab_local),
        query_spots.reshape(blocks, 2 * query_count, vocab_local),
        query_columns.reshape(blocks, 2 * query_count, query_length, -1),
    )
    passage_items = (
        passage_push.reshape(blocks, 2 * passage_count, vocab_local),
        passage_spots.reshape(blocks, 2 * passage_count, vocab_local),
        passage_columns.reshape(blocks, 2 * passage_count, passage_length, -1),
    )
    query_positions = jnp.arange(query_length, dtype=jnp.int32)
    passage_positions = jnp.arange(passage_length, dtype=jnp.int32)
    contract = (((0, 1), (0, 1)), ((), ()))

    def accumulate(running, block_items):
        query_block, query_spot, query_rows, passage_block, passage_spot, passage_rows = block_items
        query_table = spread(query_block, query_spot, query_positions)
        passage_table = spread(passage_block, passage_spot, passage_positions)
        running = running + lax.dot_general(
            query_table, query_rows, contract, preferred_element_type=jnp.float32
        )
        running = running + lax.dot_general(
            passage_table, passage_rows, contract, preferred_element_type=jnp.float32
        )
        return (running, None)

    initial = jnp.zeros((vocab_local, head_weight.shape[1]), jnp.float32)
    weight_grad, block_parts = lax.scan(accumulate, initial, query_items + passage_items)
    own_group = lax.axis_index("dp")
    own_query = spread(
        lax.dynamic_slice_in_dim(query_push, own_group * query_count, query_count, 0),
        query_where,
        query_positions,
    )
    own_passage = spread(
        lax.dynamic_slice_in_dim(passage_push, own_group * passage_count, passage_count, 0),
        passage_where,
        passage_positions,
    )
    stacked = jnp.concatenate(
        [own_query.reshape(-1, vocab_local), own_passage.reshape(-1, vocab_local)], axis=0
    )
    rows_all = jnp.dot(
        stacked,
        lax.all_gather(head_weight, "dp", axis=1, tiled=True),
        preferred_element_type=jnp.float32,
    ).astype(jnp.bfloat16)
    split_at = query_count * query_length
    query_parts = rows_all[:split_at].reshape(query_count, query_length, -1)
    passage_parts = rows_all[split_at:].reshape(passage_count, passage_length, -1)
    query_sum, passage_sum = (
        lax.psum_scatter(query_parts, "vocab", scatter_dimension=2, tiled=True).astype(jnp.float32),
        lax.psum_scatter(passage_parts, "vocab", scatter_dimension=2, tiled=True).astype(
            jnp.float32
        ),
    )
    return (query_sum.astype(jnp.bfloat16), passage_sum.astype(jnp.bfloat16), weight_grad)


def solution(mesh):
    in_specs = (
        P("dp", None, None),
        P("dp", None, None),
        P("dp", None, "vocab"),
        P("dp", None, "vocab"),
        P("vocab", "dp"),
        P("dp", None),
        P("dp", None),
        P(),
        P(),
    )
    out_specs = (P("dp", None, "vocab"), P("dp", None, "vocab"), P("vocab", "dp"))
    return jax.shard_map(
        on_device, mesh=mesh, in_specs=in_specs, out_specs=out_specs, check_vma=False
    )
```

profile of v0, /device:TPU:6, one launch (start us, length us, event | category | flops | bytes accessed | tf_op | source)
XLA Modules:
  0.0 304.4 jit_solution(2272215180256723581)
XLA Ops:
  7.9 4.9 %copy.14 = bf16[2,32,4096]{1,0,2:T(2,128)(2,1)S(1)} copy(bf16[2,32,4096]{2,1,0:T(8,128)(2,1)} %param.11) | data formatting | bytes 1048576 | tf_op args[0]
  12.8 2.7 reshape.113
  15.5 9.6 %all-to-all-start = ((bf16[32,2,4096]{2,1,0:T(2,128)(2,1)}), bf16[32,2,4096]{2,1,0:T(2,128)(2,1)S(1)}, u32[]{:S(2)}, u32[]{:S(2)}) async-start(bf16[32,2,4096]{2,1,0:T(2,128)(2,1)} %reshape.113), calls=%async_computation.2 | async-start | bytes 1048576 | tf_op jit(solution)/shard_map/all_to_all | solution.py:62
  25.7 25.2 %all-gather.1 = f32[32,2,1024]{2,1,0:T(2,128)S(1)} all-gather(f32[1,2,1024]{2,1,0:T(2,128)S(1)} %bitcast.76), channel_id=1, replica_groups=mesh['dp'=32,'vocab'=16] {'dp'}, dimensions={0}, use_global_device_ids=true | all-gather | bytes 270336 | tf_op jit(solution)/shard_map/all_gather | solution.py:67
  51.3 24.1 %all-gather = f32[32,2,1024]{2,1,0:T(2,128)S(1)} all-gather(f32[1,2,1024]{2,1,0:T(2,128)S(1)} %bitcast.77), channel_id=1, replica_groups=mesh['dp'=32,'vocab'=16] {'dp'}, dimensions={0}, use_global_device_ids=true | all-gather | bytes 270336 | tf_op jit(solution)/shard_map/all_gather | solution.py:66
  75.4 1.7 maximum_log-plus-one_fusion
  79.6 4.0 %copy.16 = bf16[2,96,4096]{1,0,2:T(2,128)(2,1)} copy(bf16[2,96,4096]{2,1,0:T(8,128)(2,1)S(1)} %copy-done.3) | data formatting | bytes 3145728 | tf_op args[1]
  84.0 60.8 %psum.7 = f32[64,64]{1,0:T(8,128)S(1)} all-reduce(f32[64,64]{1,0:T(8,128)S(1)} %fusion.41), channel_id=1, replica_groups=mesh['dp'=32,'vocab'=16] {'vocab'}, use_global_device_ids=true, to_apply=%region_2.3 | all-reduce | flops 4096 | bytes 32768 | tf_op jit(solution)/shard_map/psum | solution.py:75
  146.4 6.4 %all-to-all-start.1 = ((bf16[2,96,4096]{1,0,2:T(2,128)(2,1)}), bf16[2,96,4096]{1,0,2:T(2,128)(2,1)}, u32[]{:S(2)}, u32[]{:S(2)}) async-start(bf16[2,96,4096]{1,0,2:T(2,128)(2,1)} %copy.16), calls=%async_computation.3 | async-start | bytes 4194304 | tf_op jit(solution)/shard_map/all_to_all | solution.py:63
  153.0 5.7 %convolution_convert_fusion = bf16[256,4096]{1,0:T(8,128)(2,1)S(1)} fusion(bf16[1024,4096]{1,0:T(8,128)(2,1)} %all-gather.6.cloned.1.call-done, bf16[192,1024]{1,0:T(8,128)(2,1)S(1)} %fusion.32, bf16[64,1024]{1,0:T(8,128)(2,1)S(1)} %fusion.36), kind=kOutput, calls=%fused_computation.28 | convolution fusion | flops 2149580800 | bytes 11010048 | tf_op jit(solution)/shard_map/dot_general | solution.py:134
  158.8 1.3 copy-done.1
  161.8 33.8 %all-gather.2 = s32[32,2,1024]{2,1,0:T(2,128)S(1)} all-gather(s32[1,2,1024]{2,1,0:T(2,128)S(1)} %bitcast.75), channel_id=1, replica_groups=mesh['dp'=32,'vocab'=16] {'dp'}, dimensions={0}, use_global_device_ids=true | all-gather | bytes 270336 | tf_op jit(solution)/shard_map/all_gather | solution.py:68
  195.9 23.1 %all-gather.3 = s32[32,2,1024]{2,1,0:T(2,128)S(1)} all-gather(s32[1,2,1024]{2,1,0:T(2,128)S(1)} %bitcast.74), channel_id=1, replica_groups=mesh['dp'=32,'vocab'=16] {'dp'}, dimensions={0}, use_global_device_ids=true | all-gather | bytes 270336 | tf_op jit(solution)/shard_map/all_gather | solution.py:69
  220.9 3.6 %copy.15 = bf16[32,2,32,128]{3,2,1,0:T(8,128)(2,1)} copy(bf16[32,2,32,128]{2,1,3,0:T(2,128)(2,1)S(1)} %bitcast.68) | data formatting | bytes 1048576 | tf_op jit(solution)/shard_map/all_to_all | solution.py:62
  224.6 5.6 %copy.17 = bf16[32,2,96,128]{3,2,1,0:T(8,128)(2,1)} copy(bf16[32,2,96,128]{2,1,3,0:T(2,128)(2,1)} %bitcast.15) | data formatting | bytes 3145728 | tf_op jit(solution)/shard_map/all_to_all | solution.py:63
  231.5 62.1 %while.11 = (s32[]{:T(128)}, f32[1024,128]{1,0:T(8,128)S(1)}, s32[16,4,1024]{2,1,0:T(4,128)S(1)}, bf16[16,4,1024]{2,1,0:T(4,128)(2,1)S(1)}, bf16[16,4,32,128]{3,...) while((s32[]{:T(128)}, f32[1024,128]{1,0:T(8,128)S(1)}, ...), condition=%wide.region_10.11_spmd.clone, body=%wide.region_9.10_spmd.clone.sunk | while | flops 135659520 | bytes 2375815 | solution.py:119
  248.5 1.3 convolution_bitcast_fusion.3
  252.4 1.3 convolution_bitcast_fusion.3
  256.3 1.3 convolution_bitcast_fusion.3
  275.7 1.3 convolution_bitcast_fusion.3
  279.5 1.3 convolution_bitcast_fusion.3
  283.4 1.3 convolution_bitcast_fusion.3
  291.2 1.3 convolution_bitcast_fusion.3
  293.7 4.3 %reduce-scatter.5.cloned.1.call-done = bf16[2,96,256]{2,1,0:T(8,128)(2,1)} async-done(((bf16[2,96,4096]{2,1,0:T(8,128)(2,1)}), bf16[2,96,256]{2,1,0:T(8,128)(2,1)}) %reduce-scatter.5.cloned.1.call-update) | async-done | bytes 98320 | tf_op jit(solution)/shard_map/reduce_scatter | solution.py:144
  (115 shorter events, 63.1 us)
Async XLA Ops:
  7.2 145.9 %all-gather.6.cloned.1.call-start = ((), (), s32[]{:S(2)}) async-start(), calls=%async_computation.4 | async-start | bytes 8650752 | tf_op jit(solution)/shard_map/all_gather | solution.py:136
  12.8 12.4 %copy-start.7 = (s32[2,96]{1,0:T(2,128)S(1)}, s32[2,96]{1,0:T(2,128)}, u32[]{:S(2)}) copy-start(s32[2,96]{1,0:T(2,128)} %param.17) | copy-start | bytes 2308
  12.8 12.4 %copy-start.4 = (f32[2,96,1024]{2,1,0:T(8,128)S(1)}, f32[2,96,1024]{2,1,0:T(8,128)}, u32[]{:S(2)}) copy-start(f32[2,96,1024]{2,1,0:T(8,128)} %param.14) | copy-start | bytes 2359300
  12.8 38.1 %copy-start.8 = (s32[2,32]{1,0:T(2,128)S(1)}, s32[2,32]{1,0:T(2,128)}, u32[]{:S(2)}) copy-start(s32[2,32]{1,0:T(2,128)} %param.16) | copy-start | bytes 772
  12.8 38.1 %copy-start.5 = (f32[2,32,1024]{2,1,0:T(8,128)S(1)}, f32[2,32,1024]{2,1,0:T(8,128)}, u32[]{:S(2)}) copy-start(f32[2,32,1024]{2,1,0:T(8,128)} %param.13) | copy-start | bytes 786436
  15.5 130.8 %all-to-all-start = ((bf16[32,2,4096]{2,1,0:T(2,128)(2,1)}), bf16[32,2,4096]{2,1,0:T(2,128)(2,1)S(1)}, u32[]{:S(2)}, u32[]{:S(2)}) async-start(bf16[32,2,4096]{2,1,0:T(2,128)(2,1)} %reshape.113), calls=%async_computation.2 | async-start | bytes 1048576 | tf_op jit(solution)/shard_map/all_to_all | solution.py:62
  51.0 28.6 %copy-start.3 = (bf16[2,96,4096]{2,1,0:T(8,128)(2,1)S(1)}, bf16[2,96,4096]{2,1,0:T(8,128)(2,1)}, u32[]{:S(2)}) copy-start(bf16[2,96,4096]{2,1,0:T(8,128)(2,1)} %param.12) | copy-start | bytes 4718596
  79.6 65.4 %copy-start.6 = (s32[64]{0:T(128)S(1)}, s32[64]{0:T(128)}, u32[]{:S(2)}) copy-start(s32[64]{0:T(128)} %param.18) | copy-start | bytes 772
  146.4 78.2 %all-to-all-start.1 = ((bf16[2,96,4096]{1,0,2:T(2,128)(2,1)}), bf16[2,96,4096]{1,0,2:T(2,128)(2,1)}, u32[]{:S(2)}, u32[]{:S(2)}) async-start(bf16[2,96,4096]{1,0,2:T(2,128)(2,1)} %copy.16), calls=%async_computation.3 | async-start | bytes 4194304 | tf_op jit(solution)/shard_map/all_to_all | solution.py:63
  152.8 140.9 %reduce-scatter.3.cloned.1.call-start = ((), (), s32[]{:S(2)}) async-start(), calls=%async_computation.5 | async-start | bytes 557056 | tf_op jit(solution)/shard_map/reduce_scatter | solution.py:143
  158.8 1.4 copy-start.1
  161.0 136.9 %reduce-scatter.5.cloned.1.call-start = ((), (), s32[]{:S(2)}) async-start(), calls=%async_computation.6 | async-start | bytes 1671168 | tf_op jit(solution)/shard_map/reduce_scatter | solution.py:144
  224.6 5.7 %copy-start.2 = (bf16[256,4096]{1,0:T(8,128)(2,1)S(1)}, bf16[256,4096]{1,0:T(8,128)(2,1)}, u32[]{:S(2)}) copy-start(bf16[256,4096]{1,0:T(8,128)(2,1)} %copy-done.1) | copy-start | bytes 6291460
  293.6 4.3 %copy-start = (f32[1024,128]{1,0:T(8,128)}, f32[1024,128]{1,0:T(8,128)S(1)}, u32[]{:S(2)}) copy-start(f32[1024,128]{1,0:T(8,128)S(1)} %get-tuple-element.60) | copy-start | bytes 1572868
Sparse Core Ops, SparseCore 0:
  11.1 78.9 all-gather.5
  161.1 63.6 reduce-scatter.2
  231.7 66.2 reduce-scatter.4
where the time goes:
time: 309 us; the launch traced here: 304 us
  blocking collectives  167 us (54%)
  local copies, waits for them, and re-layouts  52 us (17%)
  matrix products  45.7 us (15%)
  starting transfers between devices  16.3 us (5%)
  between operations  14.7 us (5%)
  waiting for transfers between devices  5.01 us (2%)
  other arithmetic  3.12 us (1%)
    psum x1, blocking collectives, on_device(): scores = lax.psum(partial_value, 'vocab') * factor  60.8 us
    all_gather x1, blocking collectives, on_device(): lax.all_gather(query_where, 'dp', axis=0, tiled=True)  33.8 us
    all_gather x1, blocking collectives, on_device(): lax.all_gather(passage_pool, 'dp', axis=0, tiled=True)  25.2 us
    all_gather x1, blocking collectives, on_device(): lax.all_gather(query_pool, 'dp', axis=0, tiled=True)  24.1 us
    all_gather x1, blocking collectives, on_device(): lax.all_gather(passage_where, 'dp', axis=0, tiled=True)  23.1 us
    dot_general x16, matrix products, accumulate(): lax.dot_general(passage_table, passage_rows, contract, preferred_element_...  20.9 us
    dot_general x16, matrix products, accumulate(): lax.dot_general(query_table, query_rows, contract, preferred_element_type...  17.8 us
    unnamed x22, local copies, waits for them, and re-layouts  14 us
  transfers between devices with their start and end apart: 5, of which 1 were waited for; matrix products, arithmetic and copies ran while one was open for 33% of the time, Pallas kernels for 0%

commit v1 on v0

v1 whole, which is shorter than its diff:
```python
import functools

import jax
import jax.numpy as jnp
from jax import lax
from jax.experimental import pallas as pl
from jax.experimental.pallas import tpu as pltpu
from jax.sharding import PartitionSpec as P

MESH = pl.DeviceIdType.MESH
HIGHEST = lax.Precision.HIGHEST
LOSS_SCALE = 256.0
QUERY_WEIGHT = 3.0
PASSAGE_WEIGHT = 1.0
TURN = 3
F32 = jnp.float32
BF16 = jnp.bfloat16


def pooled(logits, length):
    spots = lax.broadcasted_iota(jnp.int32, logits.shape, 0).astype(F32)
    masked = jnp.where(spots < length, logits, -jnp.inf)
    largest = jnp.max(masked, axis=0, keepdims=True)
    where = jnp.min(jnp.where(masked == largest, spots, 1e9), axis=0, keepdims=True)
    return largest, where


def kernel(
    groups,
    planes,
    inverse,
    query_hidden,
    passage_hidden,
    query_logits,
    passage_logits,
    weight,
    query_mask,
    passage_mask,
    positive,
    scale,
    grad_query,
    grad_passage,
    grad_weight,
    pools,
    rep,
    push,
    part_out,
    part_in,
    part_sum,
    hidden,
    tables,
    partials,
    stage,
    inbox,
    last,
    total,
    pool_send,
    pool_recv,
    twin_send,
    twin_recv,
    one_send,
    one_recv,
    two_send,
    two_recv,
    hidden_send,
    hidden_recv,
    ring_send,
    ring_recv,
    last_send,
    last_recv,
):
    chips = groups // 2
    half = planes // 2
    query_length = query_logits.shape[1]
    passage_length = passage_logits.shape[1]
    vocab_local = query_logits.shape[2]
    query_rows = 2 * query_length
    rows = query_rows + 2 * passage_length
    width = weight.shape[1]
    queries = 2 * groups
    me = lax.axis_index("dp")
    z = lax.axis_index("vocab")
    column = lax.div(me, 2)
    core = lax.rem(me, 2)
    twin = 2 * column + 1 - core

    def ring(value, size):
        return lax.rem(value + 4 * size, size)

    def chunk_of(owner):
        return ring(column + (TURN + 1) * planes - TURN * owner, planes)

    own_chunk = chunk_of(z)
    source_plane = ring(inverse * ring(z - column, planes), planes)
    self_last = jnp.logical_and(z == column, own_chunk == column)

    barrier = pltpu.get_barrier_semaphore()

    def greet(dp_index, plane):
        pl.semaphore_signal(barrier, inc=1, device_id=(dp_index, plane), device_id_type=MESH)

    @pl.loop(1, groups)
    def _(i):
        greet(ring(me + i, groups), z)

    @pl.loop(1, planes)
    def _(i):
        greet(me, ring(z + i, planes))

    for u in range(2):
        target = 2 * own_chunk + u

        @pl.when(jnp.logical_not(jnp.logical_and(target == me, column == z)))
        def _():
            greet(target, column)

        source = 2 * z + u

        @pl.when(jnp.logical_not(jnp.logical_and(source == me, source_plane == z)))
        def _():
            greet(source, source_plane)

    def lengths(mask):
        return jnp.sum(mask[...].astype(F32), axis=1, keepdims=True)

    query_lengths = lengths(query_mask)
    passage_lengths = lengths(passage_mask)
    found = [pooled(query_logits[s], query_lengths[s : s + 1, :]) for s in range(2)]
    found += [pooled(passage_logits[s], passage_lengths[s : s + 1, :]) for s in range(2)]
    block = jnp.concatenate([f[0] for f in found] + [f[1] for f in found], axis=0)

    def slot(group):
        return pools.at[group]

    pools[me] = block

    pl.semaphore_wait(barrier, groups + planes + 2 - 2 * self_last.astype(jnp.int32))

    def pool_copy(group, target, m):
        return pltpu.make_async_remote_copy(
            src_ref=slot(group),
            dst_ref=slot(group),
            send_sem=pool_send.at[m],
            recv_sem=pool_recv.at[m],
            device_id=(target, z),
            device_id_type=MESH,
        )

    def twin_copy(group, m):
        return pltpu.make_async_remote_copy(
            src_ref=slot(group),
            dst_ref=slot(group),
            send_sem=twin_send.at[m],
            recv_sem=twin_recv.at[m],
            device_id=(twin, z),
            device_id_type=MESH,
        )

    @pl.loop(1, chips)
    def _(m):
        pool_copy(me, 2 * ring(column + m, chips) + core, m).start()

    twin_copy(me, 0).start()

    @pl.loop(1, chips)
    def _(m):
        from_group = 2 * ring(column - m, chips) + core
        pool_copy(from_group, me, m).wait_recv()
        twin_copy(from_group, m).start()

    @pl.loop(0, chips)
    def _(m):
        twin_copy(2 * ring(column - m, chips) + 1 - core, m).wait_recv()

    def pool_rows(k):
        return pools[:, k, :]

    for k in range(4):
        rep[k * groups : (k + 1) * groups, :] = jnp.log1p(jnp.maximum(pool_rows(k), 0.0))
    part = lax.dot_general(
        rep[0:queries, :],
        rep[...],
        (((1,), (1,)), ((), ())),
        precision=HIGHEST,
        preferred_element_type=F32,
    )
    share = queries // planes
    part_out[...] = jnp.zeros_like(part_out)
    for b in range(planes):
        part_out[8 * b : 8 * b + share, :] = part[b * share : (b + 1) * share, :]

    def tile(ref, plane):
        return ref.at[pl.ds(pl.multiple_of(plane * 8, 8), 8)]

    def one_copy(plane, i):
        return pltpu.make_async_remote_copy(
            src_ref=tile(part_out, plane),
            dst_ref=tile(part_in, z),
            send_sem=one_send.at[i],
            recv_sem=one_recv.at[i],
            device_id=(me, plane),
            device_id_type=MESH,
        )

    def two_copy(plane, i):
        return pltpu.make_async_remote_copy(
            src_ref=tile(part_sum, z),
            dst_ref=tile(part_sum, z),
            send_sem=two_send.at[i],
            recv_sem=two_recv.at[i],
            device_id=(me, plane),
            device_id_type=MESH,
        )

    @pl.loop(1, planes)
    def _(i):
        one_copy(ring(z + i, planes), i).start()

    def owner_at(j):
        i = lax.div(j + 1, 2)
        sign = 2 * lax.rem(j, 2) - 1
        return ring(z + sign * (half - i), planes)

    def hidden_parts(j, cr, target):
        out = []
        columns = pl.ds(pl.multiple_of(target * width, width), width)
        for p, (source, start, count) in enumerate(
            ((query_hidden, 0, query_rows), (passage_hidden, query_rows, rows - query_rows))
        ):
            first = pl.multiple_of(me * rows + start, 64)
            out.append(
                (
                    source.at[:, columns],
                    hidden.at[pl.ds(first, count)],
                    hidden_send.at[(2 * j + cr) * 2 + p],
                    hidden_recv.at[me * 2 + p],
                )
            )
        return out

    def hidden_target(j, cr):
        return 2 * ring(column + TURN * owner_at(j), planes) + cr

    def send_hidden(j):
        for cr in range(2):
            target = hidden_target(j, cr)

            @pl.when(target != me)
            def _():
                for source, dest, send, recv in hidden_parts(j, cr, target):
                    pltpu.make_async_remote_copy(
                        src_ref=source,
                        dst_ref=dest,
                        send_sem=send,
                        recv_sem=recv,
                        device_id=(target, z),
                        device_id_type=MESH,
                    ).start()

            @pl.when(target == me)
            def _():
                for source, dest, _, recv in hidden_parts(j, cr, target):
                    pltpu.make_async_copy(source, dest, recv).start()

    @pl.loop(0, planes // 2)
    def _(j):
        send_hidden(j)

    part_in[pl.ds(pl.multiple_of(z * 8, 8), 8), :] = part_out[
        pl.ds(pl.multiple_of(z * 8, 8), 8), :
    ]

    @pl.loop(1, planes)
    def _(i):
        one_copy(ring(z - i, planes), i).wait_recv()

    summed = part_in[0:8, :]
    for b in range(1, planes):
        summed = summed + part_in[8 * b : 8 * b + 8, :]
    part_sum[pl.ds(pl.multiple_of(z * 8, 8), 8), :] = summed

    @pl.loop(1, planes)
    def _(i):
        two_copy(ring(z + i, planes), i).start()

    @pl.loop(planes // 2, planes)
    def _(j):
        send_hidden(j)

    @pl.loop(1, planes)
    def _(i):
        two_copy(ring(z - i, planes), i).wait_recv()

    factor = scale[0] / (vocab_local * planes)
    sums = jnp.concatenate([part_sum[8 * b : 8 * b + share, :] for b in range(planes)], axis=0)
    lane = lax.broadcasted_iota(jnp.int32, sums.shape, 1)
    row = lax.broadcasted_iota(jnp.int32, sums.shape, 0)
    passage_lane = lane >= queries
    scores = jnp.where(passage_lane, sums * factor, -jnp.inf)
    weights = jnp.exp(scores - jnp.max(scores, axis=1, keepdims=True))
    soft = weights / jnp.sum(weights, axis=1, keepdims=True)
    square = (queries, queries)
    square_row = lax.broadcasted_iota(jnp.int32, square, 0)
    square_lane = lax.broadcasted_iota(jnp.int32, square, 1)
    query_of_row = jnp.where(square_row < groups, 2 * square_row, 2 * (square_row - groups) + 1)
    wanted = jnp.sum(
        jnp.where(
            square_lane == query_of_row,
            jnp.broadcast_to(positive[...].astype(F32), square),
            0.0,
        ),
        axis=1,
        keepdims=True,
    )
    passage_of_lane = jnp.where(
        lane < queries + groups, 2 * (lane - queries), 2 * (lane - queries - groups) + 1
    ).astype(F32)
    target_mark = jnp.where(jnp.logical_and(passage_lane, passage_of_lane == wanted), 1.0, 0.0)
    excess = soft - target_mark
    corner = jnp.concatenate([excess, jnp.zeros_like(excess)], axis=0)
    full_row = lax.broadcasted_iota(jnp.int32, corner.shape, 0)
    full_lane = lax.broadcasted_iota(jnp.int32, corner.shape, 1)
    query_part = jnp.logical_and(full_row < queries, full_lane < queries)
    passage_part = jnp.logical_and(full_row >= queries, full_lane >= queries)
    means = jnp.where(
        query_part,
        2.0 * QUERY_WEIGHT / queries / queries,
        jnp.where(passage_part, 2.0 * PASSAGE_WEIGHT / queries / queries, 0.0),
    )
    mixing = LOSS_SCALE * (factor * (corner + corner.T) + means)
    gradient = jnp.dot(mixing, rep[...], precision=HIGHEST, preferred_element_type=F32)
    for k in range(4):
        pool = pool_rows(k)
        slope = jnp.where(pool > 0.0, 1.0 / (1.0 + jnp.maximum(pool, 0.0)), 0.0)
        pushed = gradient[k * groups : (k + 1) * groups, :] * slope
        push[k * groups : (k + 1) * groups, :] = pushed.astype(BF16).astype(F32)

    def spread(group):
        first = pl.multiple_of(group * rows, 64)
        start = 0
        for k in range(4):
            length = query_length if k < 2 else passage_length
            push_row = push[pl.ds(k * groups + group, 1), :]
            spot_row = pools[group, 4 + k : 5 + k, :]
            positions = lax.broadcasted_iota(jnp.int32, (length, vocab_local), 0).astype(F32)
            tables[pl.ds(first + start, length), :] = jnp.where(
                positions == spot_row, push_row, 0.0
            ).astype(BF16)
            start += length
        return jnp.dot(
            tables[pl.ds(first, rows), :], weight[...], preferred_element_type=F32
        )

    def place(way, step, u):
        return (way * half + step) * 2 + u

    def ring_copy(way, step, u):
        index = place(way, step, u)
        neighbour = ring(z + 1 - 2 * way, planes)
        return pltpu.make_async_remote_copy(
            src_ref=stage.at[index],
            dst_ref=inbox.at[index],
            send_sem=ring_send.at[index],
            recv_sem=ring_recv.at[index],
            device_id=(me, neighbour),
            device_id_type=MESH,
        )

    def owner_of(way, step):
        return ring(z + (1 - 2 * way) * (half - step), planes)

    def ring_step(step, chains):
        for n, (way, u, _) in enumerate(chains):
            partials[n] = spread(2 * chunk_of(owner_of(way, step)) + u)
        for n, (way, u, follows) in enumerate(chains):
            value = partials[n]
            if follows:
                ring_copy(way, step - 1, u).wait_recv()
                value = value + inbox[place(way, step - 1, u)].astype(F32)
            stage[place(way, step, u)] = value.astype(BF16)
            ring_copy(way, step, u).start()

    def add_weight(owner):
        chunk = chunk_of(owner)

        for u in range(2):
            group = 2 * chunk + u
            for p, (start, count) in enumerate(((0, query_rows), (query_rows, rows - query_rows))):
                landed = hidden.at[pl.ds(pl.multiple_of(group * rows + start, 64), count)]
                pltpu.make_async_copy(landed, landed, hidden_recv.at[group * 2 + p]).wait()
        first = pl.multiple_of(chunk * 2 * rows, 64)
        total[...] += lax.dot_general(
            hidden[pl.ds(first, 2 * rows), :],
            tables[pl.ds(first, 2 * rows), :],
            (((0,), (0,)), ((), ())),
            preferred_element_type=F32,
        )

    total[...] = jnp.zeros_like(total)
    ring_step(0, ((0, 0, False), (1, 1, False)))
    ring_step(1, ((0, 0, True), (1, 1, True), (0, 1, False), (1, 0, False)))

    @pl.loop(2, half)
    def _(step):
        ring_step(step, ((0, 0, True), (1, 1, True), (0, 1, True), (1, 0, True)))
        for way in range(2):
            add_weight(owner_of(way, step - 1))

    def last_parts(u):
        out = []
        columns = pl.ds(pl.multiple_of(core * width, width), width)
        for p, (dest, start, count) in enumerate(
            ((grad_query, 0, query_rows), (grad_passage, query_rows, rows - query_rows))
        ):
            out.append(
                (
                    last.at[u, pl.ds(start, count)],
                    dest.at[:, columns],
                    last_send.at[u * 2 + p],
                    last_recv.at[core * 2 + p],
                )
            )
        return out

    def last_remote(u):
        return [
            pltpu.make_async_remote_copy(
                src_ref=source,
                dst_ref=dest,
                send_sem=send,
                recv_sem=recv,
                device_id=(2 * own_chunk + u, column),
                device_id_type=MESH,
            )
            for source, dest, send, recv in last_parts(u)
        ]

    def to_self(u):
        return jnp.logical_and(2 * own_chunk + u == me, column == z)

    for u in range(2):
        partials[u] = spread(2 * own_chunk + u)
    for u in range(2):
        value = partials[u]
        for way in range(2):
            ring_copy(way, half - 1, u).wait_recv()
            value = value + inbox[place(way, half - 1, u)].astype(F32)
        last[u] = value.astype(BF16)

        @pl.when(jnp.logical_not(to_self(u)))
        def _():
            for copy in last_remote(u):
                copy.start()

        @pl.when(to_self(u))
        def _():
            for source, dest, _, recv in last_parts(u):
                pltpu.make_async_copy(source, dest, recv).start()

    for way in range(2):
        add_weight(owner_of(way, half - 1))
    add_weight(owner_of(0, 0))
    add_weight(z)
    grad_weight[...] = total[...].T

    for h in range(2):
        columns = pl.ds(h * width, width)
        for p, (dest, count) in enumerate(
            ((grad_query, query_rows), (grad_passage, rows - query_rows))
        ):
            landed = dest.at[:, columns]
            pltpu.make_async_copy(landed, landed, last_recv.at[h * 2 + p]).wait()
    for u in range(2):

        @pl.when(jnp.logical_not(to_self(u)))
        def _():
            for copy in last_remote(u):
                copy.wait_send()

    for way in range(2):
        for u in range(2):

            @pl.loop(0 if way == u else 1, half)
            def _(step):
                ring_copy(way, step, u).wait_send()

    @pl.loop(0, planes)
    def _(j):
        for cr in range(2):
            target = hidden_target(j, cr)

            @pl.when(target != me)
            def _():
                for source, dest, send, recv in hidden_parts(j, cr, target):
                    pltpu.make_async_remote_copy(
                        src_ref=source,
                        dst_ref=dest,
                        send_sem=send,
                        recv_sem=recv,
                        device_id=(target, z),
                        device_id_type=MESH,
                    ).wait_send()

    @pl.loop(1, planes)
    def _(i):
        one_copy(ring(z + i, planes), i).wait_send()
        two_copy(ring(z + i, planes), i).wait_send()

    @pl.loop(1, chips)
    def _(m):
        pool_copy(me, 2 * ring(column + m, chips) + core, m).wait_send()

    @pl.loop(0, chips)
    def _(m):
        twin_copy(me, m).wait_send()


def on_device(
    groups,
    planes,
    query_hidden,
    passage_hidden,
    query_logits,
    passage_logits,
    head_weight,
    query_mask,
    passage_mask,
    positive,
    score_scale,
):
    width = query_hidden.shape[2]
    query_rows = query_hidden.shape[0] * query_hidden.shape[1]
    passage_rows = passage_hidden.shape[0] * passage_hidden.shape[1]
    rows = query_rows + passage_rows
    vocab_local, block = head_weight.shape
    chips = groups // 2
    half = planes // 2
    sequences = 4 * groups
    inverse = pow(TURN, -1, planes)
    vmem = pl.BlockSpec(memory_space=pltpu.VMEM)
    anywhere = pl.BlockSpec(memory_space=pl.ANY)
    units = 4 * half
    dma = pltpu.SemaphoreType.DMA
    grad_query, grad_passage, grad_weight = pl.pallas_call(
        functools.partial(kernel, groups, planes, inverse),
        out_shape=(
            jax.ShapeDtypeStruct((query_rows, 2 * block), BF16),
            jax.ShapeDtypeStruct((passage_rows, 2 * block), BF16),
            jax.ShapeDtypeStruct((vocab_local, block), F32),
        ),
        in_specs=[anywhere] * 2 + [vmem] * 6 + [pl.BlockSpec(memory_space=pltpu.SMEM)],
        out_specs=(anywhere, anywhere, vmem),
        scratch_shapes=[
            pltpu.VMEM((groups, 8, vocab_local), F32),
            pltpu.VMEM((sequences, vocab_local), F32),
            pltpu.VMEM((sequences, vocab_local), F32),
            pltpu.VMEM((8 * planes, sequences), F32),
            pltpu.VMEM((8 * planes, sequences), F32),
            pltpu.VMEM((8 * planes, sequences), F32),
            pltpu.VMEM((groups * rows, block), BF16),
            pltpu.VMEM((groups * rows, vocab_local), BF16),
            pltpu.VMEM((4, rows, block), F32),
            pltpu.VMEM((units, rows, block), BF16),
            pltpu.VMEM((units, rows, block), BF16),
            pltpu.VMEM((2, rows, block), BF16),
            pltpu.VMEM((block, vocab_local), F32),
            dma((chips,)),
            dma((chips,)),
            dma((chips,)),
            dma((chips,)),
            dma((planes,)),
            dma((planes,)),
            dma((planes,)),
            dma((planes,)),
            dma((4 * planes,)),
            dma((2 * groups,)),
            dma((units,)),
            dma((units,)),
            dma((4,)),
            dma((4,)),
        ],
        compiler_params=pltpu.CompilerParams(
            collective_id=0, has_side_effects=True, vmem_limit_bytes=48 * 1024 * 1024
        ),
    )(
        query_hidden.reshape(query_rows, width),
        passage_hidden.reshape(passage_rows, width),
        query_logits,
        passage_logits,
        head_weight,
        query_mask,
        passage_mask,
        positive.reshape(1, -1),
        score_scale,
    )
    return (
        grad_query.reshape(query_hidden.shape[:2] + (2 * block,)),
        grad_passage.reshape(passage_hidden.shape[:2] + (2 * block,)),
        grad_weight,
    )


def solution(mesh):
    in_specs = (
        P("dp", None, None),
        P("dp", None, None),
        P("dp", None, "vocab"),
        P("dp", None, "vocab"),
        P("vocab", "dp"),
        P("dp", None),
        P("dp", None),
        P(),
        P(),
    )
    out_specs = (P("dp", None, "vocab"), P("dp", None, "vocab"), P("vocab", "dp"))
    return jax.shard_map(
        functools.partial(on_device, mesh.shape["dp"], mesh.shape["vocab"]),
        mesh=mesh,
        in_specs=in_specs,
        out_specs=out_specs,
        check_vma=False,
    )
```

time: 309 us -> 116 us (0.38)
  the two profiles are of different devices: /device:TPU:6 before, /device:TPU:55 now
where the time goes in v1:
time: 116 us
  Pallas kernels  105 us (91%)
  local copies, waits for them, and re-layouts  9.54 us (8%)
  between operations  1.3 us (1%)
    pallas_call x1, Pallas kernels, on_device(): pl.pallas_call(functools.partial(kernel, groups, planes, inverse), out_sh...  105 us
    unnamed x19, local copies, waits for them, and re-layouts  9.54 us

profile of v1, /device:TPU:55, one launch (start us, length us, event | category | flops | bytes accessed | tf_op | source)
XLA Modules:
  0.0 115.8 jit_solution(9241893542637485335)
XLA Ops:
  1.3 0.0 copy-start
  1.3 1.4 %copy-done = bf16[2,96,4096]{2,1,0:T(8,128)(2,1)S(1)} copy-done((bf16[2,96,4096]{2,1,0:T(8,128)(2,1)S(1)}, bf16[2,96,4096]{2,1,0:T(8,128)(2,1)}, u32[]{:S(2)}) %copy-start) | copy-done | bytes 1572888
  2.7 0.0 copy-start.1
  2.7 1.1 copy-done.1
  3.8 0.0 copy-start.2
  3.8 1.0 copy-done.2
  4.9 0.0 copy-start.3
  4.9 0.9 copy-done.3
  5.8 0.0 copy-start.4
  5.8 0.9 copy-done.4
  6.8 0.0 copy-start.5
  6.8 0.7 copy-done.5
  7.4 0.0 copy-start.6
  7.4 0.7 copy-done.6
  8.1 0.0 copy-start.7
  8.1 0.7 copy-done.7
  8.8 105.0 %shard_map.112 = (bf16[64,256]{1,0:T(8,128)(2,1)S(1)}, bf16[192,256]{1,0:T(8,128)(2,1)S(1)}, f32[1024,128]{1,0:T(8,128)S(1)}) custom-call(bf16[64,4096]{1,0:T(8,128)(2,1)S(1)} %bitcast.6, bf16[192,4096]{1,0:T(8,128)(2,1)S(1)} %bitcast.5, f32[2,32,1024]{2,1,0:T(8,128)S(1)} %copy-done.3, f32[2,96,1024]{2,1,0:T(8,128)S(1)} %copy-done.1, ...), custom_call_target="tpu_custom_call" | custom-call | tf_op jit(solution)/shard_map/pallas_call | solution.py:544
  113.8 0.6 copy.16
  114.4 0.6 copy.17
  115.0 0.8 copy.18
Async XLA Ops:
  1.3 1.4 %copy-start = (bf16[2,96,4096]{2,1,0:T(8,128)(2,1)S(1)}, bf16[2,96,4096]{2,1,0:T(8,128)(2,1)}, u32[]{:S(2)}) copy-start(bf16[2,96,4096]{2,1,0:T(8,128)(2,1)} %param.10) | copy-start | bytes 4718596
  2.7 1.1 copy-start.1
  3.8 1.0 copy-start.2
  4.9 0.9 copy-start.3
  5.8 0.9 copy-start.4
  6.8 0.7 copy-start.5
  7.4 0.7 copy-start.6
  8.1 0.7 copy-start.7

commit v2 on v1

v2 whole, which is shorter than its diff:
```python
import functools

import jax
import jax.numpy as jnp
from jax import lax
from jax.experimental import pallas as pl
from jax.experimental.pallas import tpu as pltpu
from jax.sharding import PartitionSpec as P

MESH = pl.DeviceIdType.MESH
HIGHEST = lax.Precision.HIGHEST
LOSS_SCALE = 256.0
QUERY_WEIGHT = 3.0
PASSAGE_WEIGHT = 1.0
F32 = jnp.float32
BF16 = jnp.bfloat16


def pooled(logits, length):
    spots = lax.broadcasted_iota(jnp.int32, logits.shape, 0).astype(F32)
    masked = jnp.where(spots < length, logits, -jnp.inf)
    largest = jnp.max(masked, axis=0, keepdims=True)
    where = jnp.min(jnp.where(masked == largest, spots, 1e9), axis=0, keepdims=True)
    return largest, where


def kernel(
    groups,
    planes,
    query_hidden,
    passage_hidden,
    query_logits_in,
    passage_logits_in,
    weight_in,
    query_mask_in,
    passage_mask_in,
    positive_in,
    scale,
    grad_query,
    grad_passage,
    grad_weight,
    query_logits,
    passage_logits,
    weight,
    query_mask,
    passage_mask,
    positive,
    pools,
    spots,
    rep,
    push,
    part_out,
    part_in,
    part_sum,
    turned,
    mixed,
    hidden,
    tables,
    partial,
    stage,
    inbox,
    last,
    final,
    total,
    load,
    pool_send,
    pool_recv,
    twin_send,
    twin_recv,
    spot_send,
    spot_recv,
    spot_twin_send,
    spot_twin_recv,
    one_send,
    one_recv,
    two_send,
    two_recv,
    mixed_send,
    mixed_recv,
    hidden_send,
    hidden_recv,
    ring_send,
    ring_recv,
    last_send,
    last_recv,
):
    chips = groups // 2
    half = planes // 2
    query_length = query_logits.shape[1]
    passage_length = passage_logits.shape[1]
    vocab_local = query_logits.shape[2]
    query_rows = 2 * query_length
    rows = query_rows + 2 * passage_length
    width = weight.shape[1]
    queries = 2 * groups
    strip = 2 * width // chips
    span = rows * chips // 2
    me = lax.axis_index("dp")
    z = lax.axis_index("vocab")
    column = lax.div(me, 2)
    core = lax.rem(me, 2)
    twin = 2 * column + 1 - core

    def ring(value, size):
        return lax.rem(value + 2 * size, size)

    def remote(source, dest, send, recv, target, plane):
        return pltpu.make_async_remote_copy(
            src_ref=source,
            dst_ref=dest,
            send_sem=send,
            recv_sem=recv,
            device_id=(target, plane),
            device_id_type=MESH,
        )

    loads = [
        pltpu.make_async_copy(source, dest, load.at[n])
        for n, (source, dest) in enumerate(
            (
                (query_mask_in, query_mask),
                (passage_mask_in, passage_mask),
                (query_logits_in, query_logits),
                (passage_logits_in, passage_logits),
                (weight_in, weight),
                (positive_in, positive),
            )
        )
    ]
    for copy in loads:
        copy.start()

    barrier = pltpu.get_barrier_semaphore()

    def greet(dp_index, plane):
        pl.semaphore_signal(barrier, inc=1, device_id=(dp_index, plane), device_id_type=MESH)

    @pl.loop(1, groups)
    def _(i):
        greet(ring(me + i, groups), z)

    @pl.loop(1, planes)
    def _(i):
        greet(me, ring(z + i, planes))

    def lengths(mask):
        return jnp.sum(mask[...].astype(F32), axis=1, keepdims=True)

    for copy in loads[:4]:
        copy.wait()
    query_lengths = lengths(query_mask)
    passage_lengths = lengths(passage_mask)
    found = [pooled(query_logits[s], query_lengths[s : s + 1, :]) for s in range(2)]
    found += [pooled(passage_logits[s], passage_lengths[s : s + 1, :]) for s in range(2)]
    middle = vocab_local // 2

    def folded(lines):
        return jnp.concatenate(
            [line[:, :middle] for line in lines] + [line[:, middle:] for line in lines], axis=0
        )

    pools[me] = folded([f[0] for f in found])
    spots[me] = folded([f[1] for f in found])

    pl.semaphore_wait(barrier, groups + planes - 2)

    def plane_copy(ref, send, recv, group, target, m):
        return remote(ref.at[group], ref.at[group], send.at[m], recv.at[m], target, z)

    def pool_copy(group, target, m):
        return plane_copy(pools, pool_send, pool_recv, group, target, m)

    def pool_twin(group, m):
        return plane_copy(pools, twin_send, twin_recv, group, twin, m)

    def spot_copy(group, target, m):
        return plane_copy(spots, spot_send, spot_recv, group, target, m)

    def spot_twin(group, m):
        return plane_copy(spots, spot_twin_send, spot_twin_recv, group, twin, m)

    def spread_out(copy, twin_copy):
        @pl.loop(1, chips)
        def _(m):
            copy(me, 2 * ring(column + m, chips) + core, m).start()

        twin_copy(me, 0).start()

    def hand_on(copy, twin_copy):
        @pl.loop(1, chips)
        def _(m):
            group = 2 * ring(column - m, chips) + core
            copy(group, me, m).wait_recv()
            twin_copy(group, m).start()

    def take_from_twin(twin_copy):
        @pl.loop(0, chips)
        def _(m):
            twin_copy(2 * ring(column - m, chips) + 1 - core, m).wait_recv()

    spread_out(pool_copy, pool_twin)
    hand_on(pool_copy, pool_twin)
    spread_out(spot_copy, spot_twin)
    take_from_twin(pool_twin)

    def pool_rows(k):
        return jnp.concatenate([pools[:, k, :], pools[:, 4 + k, :]], axis=1)

    for k in range(4):
        rep[k * groups : (k + 1) * groups, :] = jnp.log1p(jnp.maximum(pool_rows(k), 0.0))
    part = lax.dot_general(
        rep[0:queries, :],
        rep[...],
        (((1,), (1,)), ((), ())),
        precision=HIGHEST,
        preferred_element_type=F32,
    )
    share = queries // chips
    part_out[...] = jnp.zeros_like(part_out)
    for b in range(chips):
        part_out[8 * b : 8 * b + share, :] = part[b * share : (b + 1) * share, :]

    def tile(ref, index):
        return ref.at[pl.ds(pl.multiple_of(index * 8, 8), 8)]

    def one_copy(plane, i):
        return remote(
            tile(part_out, column), tile(part_in, z), one_send.at[i], one_recv.at[i], me, plane
        )

    def two_copy(chip, i):
        return remote(
            tile(part_sum, column),
            tile(part_sum, column),
            two_send.at[i],
            two_recv.at[i],
            2 * chip + core,
            z,
        )

    @pl.loop(1, planes)
    def _(i):
        one_copy(ring(z + i, planes), i).start()

    part_in[pl.ds(pl.multiple_of(z * 8, 8), 8), :] = part_out[
        pl.ds(pl.multiple_of(column * 8, 8), 8), :
    ]

    for copy in loads[4:]:
        copy.wait()
    turned[...] = weight[...].astype(F32).T.astype(BF16)

    def strip_rows(ref, index):
        return ref.at[pl.ds(pl.multiple_of(index * strip, strip), strip)]

    def mixed_target(i):
        chip = core * half + lax.div(i, 2)
        return 2 * ring(chip + column, half) + 2 * core * half + lax.rem(i, 2)

    def mixed_copy(i):
        target = mixed_target(i)
        return remote(
            strip_rows(turned, lax.div(target, 2) - core * half),
            strip_rows(mixed, column),
            mixed_send.at[i],
            mixed_recv.at[column],
            target,
            z,
        )

    @pl.loop(0, 2 * half)
    def _(i):
        @pl.when(mixed_target(i) != me)
        def _():
            mixed_copy(i).start()

        @pl.when(mixed_target(i) == me)
        def _():
            pltpu.make_async_copy(
                strip_rows(turned, column - core * half),
                strip_rows(mixed, column),
                mixed_recv.at[column],
            ).start()

    def hidden_parts(j, cr, target):
        out = []
        columns = pl.ds(pl.multiple_of(target * width, width), width)
        for p, (source, start, count) in enumerate(
            ((query_hidden, 0, query_rows), (passage_hidden, query_rows, rows - query_rows))
        ):
            first = pl.multiple_of(me * rows + start, 64)
            out.append(
                (
                    source.at[:, columns],
                    hidden.at[pl.ds(first, count)],
                    hidden_send.at[(2 * j + cr) * 2 + p],
                    hidden_recv.at[me * 2 + p],
                )
            )
        return out

    def hidden_target(j, cr):
        return 2 * ring(column - j, chips) + cr

    def send_hidden(j):
        for cr in range(2):
            target = hidden_target(j, cr)

            @pl.when(target != me)
            def _():
                for source, dest, send, recv in hidden_parts(j, cr, target):
                    remote(source, dest, send, recv, target, z).start()

            @pl.when(target == me)
            def _():
                for source, dest, _, recv in hidden_parts(j, cr, target):
                    pltpu.make_async_copy(source, dest, recv).start()

    @pl.loop(0, chips // 2)
    def _(j):
        send_hidden(j)

    @pl.loop(1, planes)
    def _(i):
        one_copy(ring(z - i, planes), i).wait_recv()

    summed = part_in[0:8, :]
    for b in range(1, planes):
        summed = summed + part_in[8 * b : 8 * b + 8, :]
    part_sum[pl.ds(pl.multiple_of(column * 8, 8), 8), :] = summed

    @pl.loop(1, chips)
    def _(i):
        two_copy(ring(column + i, chips), i).start()

    hand_on(spot_copy, spot_twin)

    @pl.loop(chips // 2, chips)
    def _(j):
        send_hidden(j)

    @pl.loop(1, chips)
    def _(i):
        other = ring(column - i, chips)
        remote(
            tile(part_sum, other),
            tile(part_sum, other),
            two_send.at[i],
            two_recv.at[i],
            me,
            z,
        ).wait_recv()

    factor = scale[0] / (vocab_local * planes)
    sums = jnp.concatenate([part_sum[8 * b : 8 * b + share, :] for b in range(chips)], axis=0)
    lane = lax.broadcasted_iota(jnp.int32, sums.shape, 1)
    passage_lane = lane >= queries
    scores = jnp.where(passage_lane, sums * factor, -jnp.inf)
    weights = jnp.exp(scores - jnp.max(scores, axis=1, keepdims=True))
    soft = weights / jnp.sum(weights, axis=1, keepdims=True)
    square = (queries, queries)
    square_row = lax.broadcasted_iota(jnp.int32, square, 0)
    square_lane = lax.broadcasted_iota(jnp.int32, square, 1)
    query_of_row = jnp.where(square_row < groups, 2 * square_row, 2 * (square_row - groups) + 1)
    wanted = jnp.sum(
        jnp.where(
            square_lane == query_of_row,
            jnp.broadcast_to(positive[...].astype(F32), square),
            0.0,
        ),
        axis=1,
        keepdims=True,
    )
    passage_of_lane = jnp.where(
        lane < queries + groups, 2 * (lane - queries), 2 * (lane - queries - groups) + 1
    ).astype(F32)
    target_mark = jnp.where(jnp.logical_and(passage_lane, passage_of_lane == wanted), 1.0, 0.0)
    excess = soft - target_mark
    corner = jnp.concatenate([excess, jnp.zeros_like(excess)], axis=0)
    full_row = lax.broadcasted_iota(jnp.int32, corner.shape, 0)
    full_lane = lax.broadcasted_iota(jnp.int32, corner.shape, 1)
    query_part = jnp.logical_and(full_row < queries, full_lane < queries)
    passage_part = jnp.logical_and(full_row >= queries, full_lane >= queries)
    means = jnp.where(
        query_part,
        2.0 * QUERY_WEIGHT / queries / queries,
        jnp.where(passage_part, 2.0 * PASSAGE_WEIGHT / queries / queries, 0.0),
    )
    mixing = LOSS_SCALE * (factor * (corner + corner.T) + means)
    gradient = jnp.dot(mixing, rep[...], precision=HIGHEST, preferred_element_type=F32)
    for k in range(4):
        pool = pool_rows(k)
        slope = jnp.where(pool > 0.0, 1.0 / (1.0 + jnp.maximum(pool, 0.0)), 0.0)
        pushed = gradient[k * groups : (k + 1) * groups, :] * slope
        push[k * groups : (k + 1) * groups, :] = pushed.astype(BF16).astype(F32)

    take_from_twin(spot_twin)

    @pl.loop(0, chips)
    def _(chip):
        landed = strip_rows(mixed, chip)
        pltpu.make_async_copy(landed, landed, mixed_recv.at[chip]).wait()

    def table(group):
        return tables.at[pl.ds(pl.multiple_of(group * rows, rows), rows)]

    def build(group):
        first = group * rows
        start = 0
        for k in range(4):
            length = query_length if k < 2 else passage_length
            push_row = push[pl.ds(k * groups + group, 1), :]
            spot_row = jnp.concatenate(
                [spots[group, k : k + 1, :], spots[group, 4 + k : 5 + k, :]], axis=1
            )
            positions = lax.broadcasted_iota(jnp.int32, (length, vocab_local), 0).astype(F32)
            tables[pl.ds(pl.multiple_of(first + start, 32), length), :] = jnp.where(
                positions == spot_row, push_row, 0.0
            ).astype(BF16)
            start += length

    def sum_unit(u):
        @pl.loop(u * (chips // 2), (u + 1) * (chips // 2))
        def _(j):
            group = 2 * j + core
            build(group)
            partial[:, pl.ds(pl.multiple_of(j * rows, rows), rows)] = lax.dot_general(
                mixed[...],
                table(group)[...],
                (((1,), (1,)), ((), ())),
                preferred_element_type=F32,
            )

    def own_part(plane, u):
        return partial[
            pl.ds(pl.multiple_of(plane * strip, strip), strip), u * span : (u + 1) * span
        ]

    def place(way, step, u):
        return (way * half + step) * 2 + u

    def ring_copy(way, step, u):
        index = place(way, step, u)
        neighbour = ring(z + 1 - 2 * way, planes)
        return remote(
            stage.at[index], inbox.at[index], ring_send.at[index], ring_recv.at[index], me, neighbour
        )

    def owner_of(way, step):
        return ring(z + (1 - 2 * way) * (half - step), planes)

    def ring_step(step, chains):
        for way, u, follows in chains:
            value = own_part(owner_of(way, step), u)
            if follows:
                ring_copy(way, step - 1, u).wait_recv()
                value = value + inbox[place(way, step - 1, u)].astype(F32)
            stage[place(way, step, u)] = value.astype(BF16)
            ring_copy(way, step, u).start()

    def add_weight(m):
        chip = ring(column + m, chips)
        build(2 * chip + 1 - core)
        for u in range(2):
            group = 2 * chip + u
            for p, (start, count) in enumerate(((0, query_rows), (query_rows, rows - query_rows))):
                landed = hidden.at[pl.ds(pl.multiple_of(group * rows + start, 64), count)]
                pltpu.make_async_copy(landed, landed, hidden_recv.at[group * 2 + p]).wait()
        first = pl.multiple_of(chip * 2 * rows, 64)
        total[...] += lax.dot_general(
            hidden[pl.ds(first, 2 * rows), :],
            tables[pl.ds(first, 2 * rows), :],
            (((0,), (0,)), ((), ())),
            preferred_element_type=F32,
        )

    sum_unit(0)
    ring_step(0, ((0, 0, False),))
    sum_unit(1)
    ring_step(0, ((1, 1, False),))
    ring_step(1, ((0, 0, True), (1, 0, False), (0, 1, False), (1, 1, True)))
    total[...] = jnp.zeros_like(total)

    @pl.loop(2, half)
    def _(step):
        ring_step(step, ((0, 0, True), (1, 0, True), (0, 1, True), (1, 1, True)))
        for i in range(2):
            add_weight(2 * (step - 2) + i)

    def last_copy(j, target):
        return remote(
            last.at[:, pl.ds(pl.multiple_of(j * rows, rows), rows)],
            strip_rows(final, column),
            last_send.at[j],
            last_recv.at[column],
            target,
            z,
        )

    for u in range(2):
        value = own_part(z, u)
        for way in range(2):
            ring_copy(way, half - 1, u).wait_recv()
            value = value + inbox[place(way, half - 1, u)].astype(F32)
        last[:, u * span : (u + 1) * span] = value.astype(BF16)

        @pl.loop(u * (chips // 2), (u + 1) * (chips // 2))
        def _(j):
            @pl.when(j != column)
            def _():
                last_copy(j, 2 * j + core).start()

            @pl.when(j == column)
            def _():
                pltpu.make_async_copy(
                    last.at[:, pl.ds(pl.multiple_of(j * rows, rows), rows)],
                    strip_rows(final, column),
                    last_recv.at[column],
                ).start()

    @pl.loop(2 * (half - 2), chips)
    def _(m):
        add_weight(m)

    grad_weight[...] = total[...].T

    @pl.loop(0, chips)
    def _(chip):
        landed = strip_rows(final, chip)
        pltpu.make_async_copy(landed, landed, last_recv.at[chip]).wait()

    whole = final[...].astype(F32).T.astype(BF16)
    grad_query[...] = whole[:query_rows, :]
    grad_passage[...] = whole[query_rows:, :]

    @pl.loop(0, chips)
    def _(j):
        @pl.when(j != column)
        def _():
            last_copy(j, 2 * j + core).wait_send()

    for way in range(2):
        for u in range(2):

            @pl.loop(0 if way == u else 1, half)
            def _(step):
                ring_copy(way, step, u).wait_send()

    @pl.loop(0, chips)
    def _(j):
        for cr in range(2):
            target = hidden_target(j, cr)

            @pl.when(target != me)
            def _():
                for source, dest, send, recv in hidden_parts(j, cr, target):
                    remote(source, dest, send, recv, target, z).wait_send()

    @pl.loop(0, 2 * half)
    def _(i):
        @pl.when(mixed_target(i) != me)
        def _():
            mixed_copy(i).wait_send()

    @pl.loop(1, planes)
    def _(i):
        one_copy(ring(z + i, planes), i).wait_send()

    @pl.loop(1, chips)
    def _(m):
        two_copy(ring(column + m, chips), m).wait_send()
        pool_copy(me, 2 * ring(column + m, chips) + core, m).wait_send()
        spot_copy(me, 2 * ring(column + m, chips) + core, m).wait_send()

    @pl.loop(0, chips)
    def _(m):
        pool_twin(me, m).wait_send()
        spot_twin(me, m).wait_send()


def on_device(
    groups,
    planes,
    query_hidden,
    passage_hidden,
    query_logits,
    passage_logits,
    head_weight,
    query_mask,
    passage_mask,
    positive,
    score_scale,
):
    width = query_hidden.shape[2]
    query_rows = query_hidden.shape[0] * query_hidden.shape[1]
    passage_rows = passage_hidden.shape[0] * passage_hidden.shape[1]
    rows = query_rows + passage_rows
    vocab_local, block = head_weight.shape
    chips = groups // 2
    half = planes // 2
    strip = 2 * block // chips
    sequences = 4 * groups
    vmem = pl.BlockSpec(memory_space=pltpu.VMEM)
    main = pl.BlockSpec(memory_space=pltpu.HBM)
    units = 4 * half
    dma = pltpu.SemaphoreType.DMA
    grad_query, grad_passage, grad_weight = pl.pallas_call(
        functools.partial(kernel, groups, planes),
        out_shape=(
            jax.ShapeDtypeStruct((query_rows, 2 * block), BF16),
            jax.ShapeDtypeStruct((passage_rows, 2 * block), BF16),
            jax.ShapeDtypeStruct((vocab_local, block), F32),
        ),
        in_specs=[main] * 8 + [pl.BlockSpec(memory_space=pltpu.SMEM)],
        out_specs=(vmem, vmem, vmem),
        scratch_shapes=[
            pltpu.VMEM(query_logits.shape, F32),
            pltpu.VMEM(passage_logits.shape, F32),
            pltpu.VMEM(head_weight.shape, BF16),
            pltpu.VMEM(query_mask.shape, jnp.int32),
            pltpu.VMEM(passage_mask.shape, jnp.int32),
            pltpu.VMEM((1, positive.shape[0]), jnp.int32),
            pltpu.VMEM((groups, 8, vocab_local // 2), F32),
            pltpu.VMEM((groups, 8, vocab_local // 2), F32),
            pltpu.VMEM((sequences, vocab_local), F32),
            pltpu.VMEM((sequences, vocab_local), F32),
            pltpu.VMEM((8 * chips, sequences), F32),
            pltpu.VMEM((8 * planes, sequences), F32),
            pltpu.VMEM((8 * chips, sequences), F32),
            pltpu.VMEM((block, vocab_local), BF16),
            pltpu.VMEM((2 * block, vocab_local), BF16),
            pltpu.VMEM((groups * rows, block), BF16),
            pltpu.VMEM((groups * rows, vocab_local), BF16),
            pltpu.VMEM((2 * block, chips * rows), F32),
            pltpu.VMEM((units, strip, chips * rows // 2), BF16),
            pltpu.VMEM((units, strip, chips * rows // 2), BF16),
            pltpu.VMEM((strip, chips * rows), BF16),
            pltpu.VMEM((2 * block, rows), BF16),
            pltpu.VMEM((block, vocab_local), F32),
            dma((6,)),
            dma((chips,)),
            dma((chips,)),
            dma((chips,)),
            dma((chips,)),
            dma((chips,)),
            dma((chips,)),
            dma((chips,)),
            dma((chips,)),
            dma((planes,)),
            dma((planes,)),
            dma((chips,)),
            dma((chips,)),
            dma((2 * half,)),
            dma((chips,)),
            dma((4 * chips,)),
            dma((2 * groups,)),
            dma((units,)),
            dma((units,)),
            dma((chips,)),
            dma((chips,)),
        ],
        compiler_params=pltpu.CompilerParams(
            collective_id=0, has_side_effects=True, vmem_limit_bytes=60 * 1024 * 1024
        ),
    )(
        query_hidden.reshape(query_rows, width),
        passage_hidden.reshape(passage_rows, width),
        query_logits,
        passage_logits,
        head_weight,
        query_mask,
        passage_mask,
        positive.reshape(1, -1),
        score_scale,
    )
    return (
        grad_query.reshape(query_hidden.shape[:2] + (2 * block,)),
        grad_passage.reshape(passage_hidden.shape[:2] + (2 * block,)),
        grad_weight,
    )


def solution(mesh):
    in_specs = (
        P("dp", None, None),
        P("dp", None, None),
        P("dp", None, "vocab"),
        P("dp", None, "vocab"),
        P("vocab", "dp"),
        P("dp", None),
        P("dp", None),
        P(),
        P(),
    )
    out_specs = (P("dp", None, "vocab"), P("dp", None, "vocab"), P("vocab", "dp"))
    return jax.shard_map(
        functools.partial(on_device, mesh.shape["dp"], mesh.shape["vocab"]),
        mesh=mesh,
        in_specs=in_specs,
        out_specs=out_specs,
        check_vma=False,
    )
```

time: 116 us -> 127 us (1.095)
  the two profiles are of different devices: /device:TPU:55 before, /device:TPU:6 now
where the time goes in v2:
time: 127 us; the launch traced here: 126 us
  Pallas kernels  120 us (94%)
  local copies, waits for them, and re-layouts  4.78 us (4%)
  between operations  1.29 us (1%)
    pallas_call x1, Pallas kernels, on_device(): pl.pallas_call(functools.partial(kernel, groups, planes), out_shape=(jax....  120 us
    unnamed x3, local copies, waits for them, and re-layouts  4.78 us

profile of v2, /device:TPU:6, one launch (start us, length us, event | category | flops | bytes accessed | tf_op | source)
XLA Modules:
  0.0 126.3 jit_solution(7712840645600778514)
XLA Ops:
  1.3 120.2 %shard_map.112 = (bf16[64,256]{1,0:T(8,128)(2,1)}, bf16[192,256]{1,0:T(8,128)(2,1)}, f32[1024,128]{1,0:T(8,128)}) custom-call(bf16[64,4096]{1,0:T(8,128)(2,1)} %bitcast.6, bf16[192,4096]{1,0:T(8,128)(2,1)} %bitcast.5, f32[2,32,1024]{2,1,0:T(8,128)} %query_logits_in.1, f32[2,96,1024]{2,1,0:T(8,128)} %passage_logits_in.1, bf16[1024,128]{1,0:T(8,128)(2,1)} %weight_in.1, ...), custom_call_target="tpu_custom_call" | custom-call | tf_op jit(solution)/shard_map/pallas_call | solution.py:607
  121.5 1.4 %copy.16 = bf16[2,32,256]{2,1,0:T(8,128)(2,1)} copy(bf16[2,32,256]{2,1,0:T(8,128)(2,1)} %bitcast.8) | data formatting | bytes 65536
  122.9 1.5 %copy.17 = bf16[2,96,256]{2,1,0:T(8,128)(2,1)} copy(bf16[2,96,256]{2,1,0:T(8,128)(2,1)} %bitcast.7) | data formatting | bytes 196608
  124.4 1.9 %copy.18 = f32[1024,128]{1,0:T(8,128)} copy(f32[1024,128]{1,0:T(8,128)} %get-tuple-element.14) | data formatting | bytes 1048576

commit v3 on v2

v3 whole, which is shorter than its diff:
```python
import functools

import jax
import jax.numpy as jnp
from jax import lax
from jax.experimental import pallas as pl
from jax.experimental.pallas import tpu as pltpu
from jax.sharding import PartitionSpec as P

MESH = pl.DeviceIdType.MESH
HIGHEST = lax.Precision.HIGHEST
LOSS_SCALE = 256.0
QUERY_WEIGHT = 3.0
PASSAGE_WEIGHT = 1.0
F32 = jnp.float32
BF16 = jnp.bfloat16
UNITS = 4


def pooled(logits, length):
    spots = lax.broadcasted_iota(jnp.int32, logits.shape, 0).astype(F32)
    masked = jnp.where(spots < length, logits, -jnp.inf)
    largest = jnp.max(masked, axis=0, keepdims=True)
    where = jnp.min(jnp.where(masked == largest, spots, 1e9), axis=0, keepdims=True)
    return largest, where


def kernel(
    groups,
    planes,
    query_hidden,
    passage_hidden,
    query_logits_in,
    passage_logits_in,
    weight_in,
    query_mask_in,
    passage_mask_in,
    positive_in,
    scale,
    grad_query,
    grad_passage,
    grad_weight,
    query_logits,
    passage_logits,
    weight,
    query_mask,
    passage_mask,
    positive,
    pools,
    spots,
    rep,
    push,
    part_out,
    part_in,
    part_sum,
    turned,
    mixed,
    hidden,
    tables,
    partial,
    stage,
    inbox,
    last,
    final,
    total,
    load,
    sent,
    pool_recv,
    twin_recv,
    spot_recv,
    spot_twin_recv,
    one_recv,
    two_recv,
    mixed_recv,
    mixed_twin_recv,
    hidden_recv,
    ring_recv,
    last_recv,
):
    chips = groups // 2
    half = planes // 2
    query_length = query_logits.shape[1]
    passage_length = passage_logits.shape[1]
    vocab_local = query_logits.shape[2]
    query_rows = 2 * query_length
    rows = query_rows + 2 * passage_length
    width = weight.shape[1]
    queries = 2 * groups
    strip = 2 * width // chips
    span = rows * chips // UNITS
    me = lax.axis_index("dp")
    z = lax.axis_index("vocab")
    column = lax.div(me, 2)
    core = lax.rem(me, 2)
    twin = 2 * column + 1 - core
    pool_sent, twin_sent, spot_sent, spot_twin_sent, one_sent = (sent.at[i] for i in range(5))
    two_sent, mixed_sent, mixed_twin_sent, hidden_sent = (sent.at[i] for i in range(5, 9))
    ring_sent, last_sent = sent.at[9], sent.at[10]

    def ring(value, size):
        return lax.rem(value + 2 * size, size)

    def remote(source, dest, send, recv, target, plane):
        return pltpu.make_async_remote_copy(
            src_ref=source,
            dst_ref=dest,
            send_sem=send,
            recv_sem=recv,
            device_id=(target, plane),
            device_id_type=MESH,
        )

    def settle(ref, sem):
        pltpu.make_async_copy(ref, ref, sem).wait()

    loads = [
        pltpu.make_async_copy(source, dest, load.at[n])
        for n, (source, dest) in enumerate(
            (
                (query_mask_in, query_mask),
                (passage_mask_in, passage_mask),
                (query_logits_in, query_logits),
                (passage_logits_in, passage_logits),
                (weight_in, weight),
                (positive_in, positive),
            )
        )
    ]
    for copy in loads:
        copy.start()

    barrier = pltpu.get_barrier_semaphore()

    def greet(dp_index, plane):
        pl.semaphore_signal(barrier, inc=1, device_id=(dp_index, plane), device_id_type=MESH)

    @pl.loop(1, planes)
    def _(i):
        greet(me, ring(z + i, planes))

    @pl.loop(1, groups)
    def _(i):
        greet(ring(me + i, groups), z)

    def lengths(mask):
        return jnp.sum(mask[...].astype(F32), axis=1, keepdims=True)

    for copy in loads[:4]:
        copy.wait()
    query_lengths = lengths(query_mask)
    passage_lengths = lengths(passage_mask)
    found = [pooled(query_logits[s], query_lengths[s : s + 1, :]) for s in range(2)]
    found += [pooled(passage_logits[s], passage_lengths[s : s + 1, :]) for s in range(2)]
    middle = vocab_local // 2

    def folded(lines):
        return jnp.concatenate(
            [line[:, :middle] for line in lines] + [line[:, middle:] for line in lines], axis=0
        )

    pools[me] = folded([f[0] for f in found])
    spots[me] = folded([f[1] for f in found])
    for copy in loads[4:]:
        copy.wait()
    turned[...] = weight[...].astype(F32).T.astype(BF16)

    pl.semaphore_wait(barrier, groups + planes - 2)

    def pool_copy(group, target, m):
        return remote(pools.at[group], pools.at[group], pool_sent, pool_recv.at[m], target, z)

    def pool_twin(group):
        return remote(pools.at[group], pools.at[group], twin_sent, twin_recv, twin, z)

    def spot_copy(group, target, m):
        return remote(spots.at[group], spots.at[group], spot_sent, spot_recv.at[m], target, z)

    def spot_twin(group):
        return remote(spots.at[group], spots.at[group], spot_twin_sent, spot_twin_recv, twin, z)

    def spread_out(copy, twin_copy):
        @pl.loop(1, chips)
        def _(m):
            copy(me, 2 * ring(column + m, chips) + core, m).start()

        twin_copy(me).start()

    def hand_on(copy, twin_copy):
        @pl.loop(1, chips)
        def _(m):
            group = 2 * ring(column - m, chips) + core
            copy(group, me, m).wait_recv()
            twin_copy(group).start()

    spread_out(pool_copy, pool_twin)
    hand_on(pool_copy, pool_twin)

    def strip_rows(ref, index):
        return ref.at[pl.ds(pl.multiple_of(index * strip, strip), strip)]

    @pl.loop(0, half)
    def _(i):
        chip = core * half + ring(i + column, half)

        @pl.when(chip != column)
        def _():
            remote(
                strip_rows(turned, chip - core * half),
                strip_rows(mixed, column),
                mixed_sent,
                mixed_recv.at[column],
                2 * chip + core,
                z,
            ).start()

        @pl.when(chip == column)
        def _():
            pltpu.make_async_copy(
                strip_rows(turned, chip - core * half),
                strip_rows(mixed, column),
                mixed_recv.at[column],
            ).start()

    takes_strips = core == lax.div(column, half)

    def pool_rows(k):
        return jnp.concatenate([pools[:, k, :], pools[:, 4 + k, :]], axis=1)

    settle(pools.at[pl.ds(0, chips)], twin_recv)
    for k in range(4):
        rep[k * groups : (k + 1) * groups, :] = jnp.log1p(jnp.maximum(pool_rows(k), 0.0))
    part = lax.dot_general(
        rep[pl.ds(pl.multiple_of(core * groups, groups), groups), :],
        rep[queries:, :],
        (((1,), (1,)), ((), ())),
        precision=HIGHEST,
        preferred_element_type=F32,
    )
    fold = groups // 2
    part_out[...] = jnp.concatenate([part[:fold, :], part[fold:, :]], axis=1)

    @pl.loop(1, planes)
    def _(i):
        remote(part_out, part_in.at[z], one_sent, one_recv, me, ring(z + i, planes)).start()

    part_in[z] = part_out[...]
    spread_out(spot_copy, spot_twin)
    hand_on(spot_copy, spot_twin)

    @pl.when(takes_strips)
    def _():
        @pl.loop(0, chips)
        def _(chip):
            landed = strip_rows(mixed, chip)
            settle(landed, mixed_recv.at[chip])
            remote(landed, landed, mixed_twin_sent, mixed_twin_recv, twin, z).start()

    def send_hidden(j):
        for cr in range(2):
            target = 2 * ring(column - j, chips) + cr
            columns = pl.ds(pl.multiple_of(target * width, width), width)
            for source, start, count in (
                (query_hidden, 0, query_rows),
                (passage_hidden, query_rows, rows - query_rows),
            ):
                block = source.at[:, columns]
                dest = hidden.at[pl.ds(pl.multiple_of(me * rows + start, 64), count)]
                arrived = hidden_recv.at[column]

                @pl.when(target != me)
                def _():
                    remote(block, dest, hidden_sent, arrived, target, z).start()

                @pl.when(target == me)
                def _():
                    pltpu.make_async_copy(block, dest, arrived).start()

    @pl.loop(0, chips // 2)
    def _(j):
        send_hidden(j)

    settle(part_in.at[pl.ds(0, planes - 1)], one_recv)
    summed = part_in[0]
    for b in range(1, planes):
        summed = summed + part_in[b]
    part_sum[core] = summed
    swap = remote(part_sum.at[core], part_sum.at[core], two_sent, two_recv, twin, z)
    swap.start()
    swap.wait_recv()

    factor = scale[0] / (vocab_local * planes)
    sums = jnp.concatenate(
        [part_sum[k][:, h * queries : (h + 1) * queries] for k in range(2) for h in range(2)],
        axis=0,
    )
    scores = sums * factor
    weights = jnp.exp(scores - jnp.max(scores, axis=1, keepdims=True))
    soft = weights / jnp.sum(weights, axis=1, keepdims=True)
    row = lax.broadcasted_iota(jnp.int32, scores.shape, 0)
    lane = lax.broadcasted_iota(jnp.int32, scores.shape, 1)

    def natural(index):
        return jnp.where(index < groups, 2 * index, 2 * (index - groups) + 1)

    wanted = jnp.sum(
        jnp.where(
            lane == natural(row),
            jnp.broadcast_to(positive[...].astype(F32), scores.shape),
            0.0,
        ),
        axis=1,
        keepdims=True,
    )
    excess = soft - jnp.where(natural(lane).astype(F32) == wanted, 1.0, 0.0)
    nothing = jnp.zeros_like(excess)
    corner = jnp.concatenate(
        [
            jnp.concatenate([nothing, excess], axis=1),
            jnp.concatenate([nothing, nothing], axis=1),
        ],
        axis=0,
    )
    full_row = lax.broadcasted_iota(jnp.int32, corner.shape, 0)
    full_lane = lax.broadcasted_iota(jnp.int32, corner.shape, 1)
    query_part = jnp.logical_and(full_row < queries, full_lane < queries)
    passage_part = jnp.logical_and(full_row >= queries, full_lane >= queries)
    means = jnp.where(
        query_part,
        2.0 * QUERY_WEIGHT / queries / queries,
        jnp.where(passage_part, 2.0 * PASSAGE_WEIGHT / queries / queries, 0.0),
    )
    mixing = LOSS_SCALE * (factor * (corner + corner.T) + means)
    gradient = jnp.dot(mixing, rep[...], precision=HIGHEST, preferred_element_type=F32)
    for k in range(4):
        pool = pool_rows(k)
        slope = jnp.where(pool > 0.0, 1.0 / (1.0 + jnp.maximum(pool, 0.0)), 0.0)
        pushed = gradient[k * groups : (k + 1) * groups, :] * slope
        push[k * groups : (k + 1) * groups, :] = pushed.astype(BF16).astype(F32)

    settle(spots.at[pl.ds(0, chips)], spot_twin_recv)

    @pl.when(jnp.logical_not(takes_strips))
    def _():
        settle(mixed, mixed_twin_recv)

    def build(group):
        start = 0
        for k in range(4):
            length = query_length if k < 2 else passage_length
            push_row = push[pl.ds(k * groups + group, 1), :]
            spot_row = jnp.concatenate(
                [spots[group, k : k + 1, :], spots[group, 4 + k : 5 + k, :]], axis=1
            )
            positions = lax.broadcasted_iota(jnp.int32, (length, vocab_local), 0).astype(F32)
            tables[pl.ds(pl.multiple_of(group * rows + start, 32), length), :] = jnp.where(
                positions == spot_row, push_row, 0.0
            ).astype(BF16)
            start += length

    def sum_unit(u):
        @pl.loop(u * (chips // UNITS), (u + 1) * (chips // UNITS))
        def _(j):
            group = 2 * j + core
            build(group)
            partial[:, pl.ds(pl.multiple_of(j * rows, rows), rows)] = lax.dot_general(
                mixed[...],
                tables[pl.ds(pl.multiple_of(group * rows, rows), rows), :],
                (((1,), (1,)), ((), ())),
                preferred_element_type=F32,
            )

    def own_part(plane, u):
        return partial[
            pl.ds(pl.multiple_of(plane * strip, strip), strip), u * span : (u + 1) * span
        ]

    def place(way, step, u):
        return (way * half + step) * UNITS + u

    def ring_copy(way, step, u):
        index = place(way, step, u)
        neighbour = ring(z + 1 - 2 * way, planes)
        return remote(
            stage.at[index], inbox.at[index], ring_sent, ring_recv.at[index], me, neighbour
        )

    def owner_of(way, step):
        return ring(z + (1 - 2 * way) * (half - step), planes)

    def ring_step(step, way, u, follows):
        value = own_part(owner_of(way, step), u)
        if follows:
            ring_copy(way, step - 1, u).wait_recv()
            value = value + inbox[place(way, step - 1, u)].astype(F32)
        stage[place(way, step, u)] = value.astype(BF16)
        ring_copy(way, step, u).start()

    def add_weight(m):
        chip = ring(column + m, chips)
        build(2 * chip + 1 - core)
        first = pl.multiple_of(chip * 2 * rows, 64)
        settle(hidden.at[pl.ds(first, 2 * rows)], hidden_recv.at[chip])
        total[...] += lax.dot_general(
            hidden[pl.ds(first, 2 * rows), :],
            tables[pl.ds(first, 2 * rows), :],
            (((0,), (0,)), ((), ())),
            preferred_element_type=F32,
        )

    for u in range(UNITS):
        way = 0 if u < UNITS // 2 else 1
        sum_unit(u)
        ring_step(0, way, u, False)
        ring_step(1, 1 - way, u, False)
    for u in range(UNITS):
        ring_step(1, 0 if u < UNITS // 2 else 1, u, True)

    @pl.loop(chips // 2, chips)
    def _(j):
        send_hidden(j)

    total[...] = jnp.zeros_like(total)

    @pl.loop(2, half)
    def _(step):
        for u in range(UNITS):
            for way in range(2):
                ring_step(step, way, u, True)

        @pl.when(step >= 3)
        def _():
            for i in range(2):
                add_weight(2 * (step - 3) + i)

    for u in range(UNITS):
        value = own_part(z, u)
        for way in range(2):
            ring_copy(way, half - 1, u).wait_recv()
            value = value + inbox[place(way, half - 1, u)].astype(F32)
        last[:, u * span : (u + 1) * span] = value.astype(BF16)

        @pl.loop(u * (chips // UNITS), (u + 1) * (chips // UNITS))
        def _(j):
            block = last.at[:, pl.ds(pl.multiple_of(j * rows, rows), rows)]
            dest = strip_rows(final, column)

            @pl.when(j != column)
            def _():
                remote(block, dest, last_sent, last_recv, 2 * j + core, z).start()

            @pl.when(j == column)
            def _():
                pltpu.make_async_copy(block, dest, last_recv).start()

    @pl.loop(max(0, 2 * (half - 3)), chips)
    def _(m):
        add_weight(m)

    grad_weight[...] = total[...].T

    settle(final, last_recv)
    whole = final[...].astype(F32).T.astype(BF16)
    grad_query[...] = whole[:query_rows, :]
    grad_passage[...] = whole[query_rows:, :]

    settle(pools.at[pl.ds(0, chips - 1)], pool_sent)
    settle(pools.at[pl.ds(0, chips)], twin_sent)
    settle(spots.at[pl.ds(0, chips - 1)], spot_sent)
    settle(spots.at[pl.ds(0, chips)], spot_twin_sent)
    settle(part_in.at[pl.ds(0, planes - 1)], one_sent)
    swap.wait_send()

    @pl.when(takes_strips)
    def _():
        settle(mixed.at[pl.ds(0, (half - 1) * strip)], mixed_sent)
        settle(mixed, mixed_twin_sent)

    @pl.when(jnp.logical_not(takes_strips))
    def _():
        settle(mixed.at[pl.ds(0, half * strip)], mixed_sent)

    settle(hidden.at[pl.ds(0, (groups - 1) * rows)], hidden_sent)
    settle(stage.at[pl.ds(0, (2 * half - 1) * UNITS)], ring_sent)
    settle(last.at[:, pl.ds(0, (chips - 1) * rows)], last_sent)


def hand_over(*refs):
    count = (len(refs) - 1) // 2
    copies = [
        pltpu.make_async_copy(refs[n], refs[count + n], refs[-1].at[n]) for n in range(count)
    ]
    for copy in copies:
        copy.start()
    for copy in copies:
        copy.wait()


def on_device(
    groups,
    planes,
    query_hidden,
    passage_hidden,
    query_logits,
    passage_logits,
    head_weight,
    query_mask,
    passage_mask,
    positive,
    score_scale,
):
    width = query_hidden.shape[2]
    query_rows = query_hidden.shape[0] * query_hidden.shape[1]
    passage_rows = passage_hidden.shape[0] * passage_hidden.shape[1]
    rows = query_rows + passage_rows
    vocab_local, block = head_weight.shape
    chips = groups // 2
    half = planes // 2
    strip = 2 * block // chips
    sequences = 4 * groups
    vmem = pl.BlockSpec(memory_space=pltpu.VMEM)
    main = pl.BlockSpec(memory_space=pltpu.HBM)
    units = 2 * half * UNITS
    span = rows * chips // UNITS
    dma = pltpu.SemaphoreType.DMA
    grad_query, grad_passage, grad_weight = pl.pallas_call(
        functools.partial(kernel, groups, planes),
        out_shape=(
            jax.ShapeDtypeStruct((query_rows, 2 * block), BF16),
            jax.ShapeDtypeStruct((passage_rows, 2 * block), BF16),
            jax.ShapeDtypeStruct((vocab_local, block), F32),
        ),
        in_specs=[main] * 8 + [pl.BlockSpec(memory_space=pltpu.SMEM)],
        out_specs=(vmem, vmem, vmem),
        scratch_shapes=[
            pltpu.VMEM(query_logits.shape, F32),
            pltpu.VMEM(passage_logits.shape, F32),
            pltpu.VMEM(head_weight.shape, BF16),
            pltpu.VMEM(query_mask.shape, jnp.int32),
            pltpu.VMEM(passage_mask.shape, jnp.int32),
            pltpu.VMEM((1, positive.shape[0]), jnp.int32),
            pltpu.VMEM((groups, 8, vocab_local // 2), F32),
            pltpu.VMEM((groups, 8, vocab_local // 2), F32),
            pltpu.VMEM((sequences, vocab_local), F32),
            pltpu.VMEM((sequences, vocab_local), F32),
            pltpu.VMEM((chips, sequences), F32),
            pltpu.VMEM((planes, chips, sequences), F32),
            pltpu.VMEM((2, chips, sequences), F32),
            pltpu.VMEM((block, vocab_local), BF16),
            pltpu.VMEM((2 * block, vocab_local), BF16),
            pltpu.VMEM((groups * rows, block), BF16),
            pltpu.VMEM((groups * rows, vocab_local), BF16),
            pltpu.VMEM((2 * block, chips * rows), F32),
            pltpu.VMEM((units, strip, span), BF16),
            pltpu.VMEM((units, strip, span), BF16),
            pltpu.VMEM((strip, chips * rows), BF16),
            pltpu.VMEM((2 * block, rows), BF16),
            pltpu.VMEM((block, vocab_local), F32),
            dma((6,)),
            dma((11,)),
            dma((chips,)),
            dma,
            dma((chips,)),
            dma,
            dma,
            dma,
            dma((chips,)),
            dma,
            dma((chips,)),
            dma((units,)),
            dma,
        ],
        compiler_params=pltpu.CompilerParams(
            collective_id=0, has_side_effects=True, vmem_limit_bytes=60 * 1024 * 1024
        ),
    )(
        query_hidden.reshape(query_rows, width),
        passage_hidden.reshape(passage_rows, width),
        query_logits,
        passage_logits,
        head_weight,
        query_mask,
        passage_mask,
        positive.reshape(1, -1),
        score_scale,
    )
    results = (grad_query, grad_passage, grad_weight)
    grad_query, grad_passage, grad_weight = pl.pallas_call(
        hand_over,
        out_shape=tuple(jax.ShapeDtypeStruct(r.shape, r.dtype) for r in results),
        in_specs=[main] * 3,
        out_specs=(main,) * 3,
        scratch_shapes=[dma((3,))],
        compiler_params=pltpu.CompilerParams(vmem_limit_bytes=60 * 1024 * 1024),
    )(*results)
    return (
        grad_query.reshape(query_hidden.shape[:2] + (2 * block,)),
        grad_passage.reshape(passage_hidden.shape[:2] + (2 * block,)),
        grad_weight,
    )


def solution(mesh):
    in_specs = (
        P("dp", None, None),
        P("dp", None, None),
        P("dp", None, "vocab"),
        P("dp", None, "vocab"),
        P("vocab", "dp"),
        P("dp", None),
        P("dp", None),
        P(),
        P(),
    )
    out_specs = (P("dp", None, "vocab"), P("dp", None, "vocab"), P("vocab", "dp"))
    return jax.shard_map(
        functools.partial(on_device, mesh.shape["dp"], mesh.shape["vocab"]),
        mesh=mesh,
        in_specs=in_specs,
        out_specs=out_specs,
        check_vma=False,
    )
```

time: 127 us -> 98.7 us (0.78)
  Pallas kernels: 120 us -> 97.2 us
  local copies, waits for them, and re-layouts: 4.78 us -> 0 us
    pallas_call x1, Pallas kernels: 120 us -> 76.2 us  [on_device(): pl.pallas_call(functools.partial(kernel, groups, planes), out_shape=(jax....]
    pallas_call x0 -> x1, Pallas kernels: none -> 21 us  [on_device(): pl.pallas_call(hand_over, out_shape=tuple((jax.ShapeDtypeStruct(r.shape,...]
    unnamed x3 -> x0, local copies, waits for them, and re-layouts: 4.78 us -> none
where the time goes in v3:
time: 98.7 us; the launch traced here: 98.5 us
  Pallas kernels  97.2 us (98%)
  between operations  1.29 us (1%)
    pallas_call x1, Pallas kernels, on_device(): pl.pallas_call(functools.partial(kernel, groups, planes), out_shape=(jax....  76.2 us
    pallas_call x1, Pallas kernels, on_device(): pl.pallas_call(hand_over, out_shape=tuple((jax.ShapeDtypeStruct(r.shape,...  21 us

profile of v3, /device:TPU:6, one launch (start us, length us, event | category | flops | bytes accessed | tf_op | source)
XLA Modules:
  0.0 98.5 jit_solution(11213918381948255009)
XLA Ops:
  1.3 76.2 %shard_map.112 = (bf16[64,256]{1,0:T(8,128)(2,1)}, bf16[192,256]{1,0:T(8,128)(2,1)}, f32[1024,128]{1,0:T(8,128)}) custom-call(bf16[64,4096]{1,0:T(8,128)(2,1)} %bitcast.6, bf16[192,4096]{1,0:T(8,128)(2,1)} %bitcast.5, f32[2,32,1024]{2,1,0:T(8,128)} %query_logits_in.1, f32[2,96,1024]{2,1,0:T(8,128)} %passage_logits_in.1, bf16[1024,128]{1,0:T(8,128)(2,1)} %weight_in.1, ...), custom_call_target="tpu_custom_call" | custom-call | tf_op jit(solution)/shard_map/pallas_call | solution.py:525
  77.5 21.0 %shard_map.113 = (bf16[64,256]{1,0:T(8,128)(2,1)}, bf16[192,256]{1,0:T(8,128)(2,1)}, f32[1024,128]{1,0:T(8,128)}) custom-call(bf16[64,256]{1,0:T(8,128)(2,1)} %get-tuple-element.9.refs_0_, bf16[192,256]{1,0:T(8,128)(2,1)} %get-tuple-element.10.refs_1_, f32[1024,128]{1,0:T(8,128)} %get-tuple-element.11.refs_2_), custom_call_target="tpu_custom_call" | custom-call | tf_op jit(solution)/shard_map/pallas_call | solution.py:587

commit v4 on v3

--- a/solution.py
+++ b/solution.py
@@ -485,13 +485,16 @@
 
 
 def hand_over(*refs):
-    count = (len(refs) - 1) // 2
-    copies = [
-        pltpu.make_async_copy(refs[n], refs[count + n], refs[-1].at[n]) for n in range(count)
-    ]
-    for copy in copies:
+    count = (len(refs) - 1) // 3
+    sources, dests, holds = refs[:count], refs[count : 2 * count], refs[2 * count : -1]
+    arrive = [pltpu.make_async_copy(sources[n], holds[n], refs[-1].at[n]) for n in range(count)]
+    leave = [pltpu.make_async_copy(holds[n], dests[n], refs[-1].at[n]) for n in range(count)]
+    for copy in arrive:
         copy.start()
-    for copy in copies:
+    for n in range(count):
+        arrive[n].wait()
+        leave[n].start()
+    for copy in leave:
         copy.wait()
 
 
@@ -589,7 +592,7 @@
         out_shape=tuple(jax.ShapeDtypeStruct(r.shape, r.dtype) for r in results),
         in_specs=[main] * 3,
         out_specs=(main,) * 3,
-        scratch_shapes=[dma((3,))],
+        scratch_shapes=[pltpu.VMEM(r.shape, r.dtype) for r in results] + [dma((3,))],
         compiler_params=pltpu.CompilerParams(vmem_limit_bytes=60 * 1024 * 1024),
     )(*results)
     return (

time: 98.7 us -> 79.6 us (0.81)
  Pallas kernels: 97.2 us -> 78.2 us
    pallas_call x1, Pallas kernels: 21 us -> 1.93 us  [on_device(): pl.pallas_call(hand_over, out_shape=tuple((jax.ShapeDtypeStruct(r.shape,...]
where the time goes in v4:
time: 79.6 us; the launch traced here: 79.5 us
  Pallas kernels  78.2 us (98%)
  between operations  1.29 us (2%)
    pallas_call x1, Pallas kernels, on_device(): pl.pallas_call(functools.partial(kernel, groups, planes), out_shape=(jax....  76.2 us
    pallas_call x1, Pallas kernels, on_device(): pl.pallas_call(hand_over, out_shape=tuple((jax.ShapeDtypeStruct(r.shape,...  1.93 us

profile of v4, /device:TPU:6, one launch (start us, length us, event | category | flops | bytes accessed | tf_op | source)
XLA Modules:
  0.0 79.5 jit_solution(17072434304415825208)
XLA Ops:
  1.3 76.2 %shard_map.112 = (bf16[64,256]{1,0:T(8,128)(2,1)}, bf16[192,256]{1,0:T(8,128)(2,1)}, f32[1024,128]{1,0:T(8,128)}) custom-call(bf16[64,4096]{1,0:T(8,128)(2,1)} %bitcast.6, bf16[192,4096]{1,0:T(8,128)(2,1)} %bitcast.5, f32[2,32,1024]{2,1,0:T(8,128)} %query_logits_in.1, f32[2,96,1024]{2,1,0:T(8,128)} %passage_logits_in.1, bf16[1024,128]{1,0:T(8,128)(2,1)} %weight_in.1, ...), custom_call_target="tpu_custom_call" | custom-call | tf_op jit(solution)/shard_map/pallas_call | solution.py:528
  77.5 1.9 %shard_map.113 = (bf16[64,256]{1,0:T(8,128)(2,1)}, bf16[192,256]{1,0:T(8,128)(2,1)}, f32[1024,128]{1,0:T(8,128)}) custom-call(bf16[64,256]{1,0:T(8,128)(2,1)} %get-tuple-element.9.refs_0_, bf16[192,256]{1,0:T(8,128)(2,1)} %get-tuple-element.10.refs_1_, f32[1024,128]{1,0:T(8,128)} %get-tuple-element.11.refs_2_), custom_call_target="tpu_custom_call" | custom-call | tf_op jit(solution)/shard_map/pallas_call | solution.py:590

commit v5 on v4

--- a/solution.py
+++ b/solution.py
@@ -15,6 +15,7 @@
 F32 = jnp.float32
 BF16 = jnp.bfloat16
 UNITS = 4
+SLOTS = 8
 
 
 def pooled(logits, length):
@@ -113,6 +114,9 @@
     def settle(ref, sem):
         pltpu.make_async_copy(ref, ref, sem).wait()
 
+    def far_first(n, middle):
+        return middle + (1 - 2 * lax.rem(n, 2)) * lax.div(n + 1, 2)
+
     loads = [
         pltpu.make_async_copy(source, dest, load.at[n])
         for n, (source, dest) in enumerate(
@@ -134,9 +138,9 @@
     def greet(dp_index, plane):
         pl.semaphore_signal(barrier, inc=1, device_id=(dp_index, plane), device_id_type=MESH)
 
-    @pl.loop(1, planes)
-    def _(i):
-        greet(me, ring(z + i, planes))
+    @pl.loop(0, planes - 1)
+    def _(n):
+        greet(me, ring(z + far_first(n, half), planes))
 
     @pl.loop(1, groups)
     def _(i):
@@ -179,8 +183,9 @@
         return remote(spots.at[group], spots.at[group], spot_twin_sent, spot_twin_recv, twin, z)
 
     def spread_out(copy, twin_copy):
-        @pl.loop(1, chips)
-        def _(m):
+        @pl.loop(0, chips - 1)
+        def _(n):
+            m = far_first(n, chips // 2)
             copy(me, 2 * ring(column + m, chips) + core, m).start()
 
         twin_copy(me).start()
@@ -239,21 +244,13 @@
     fold = groups // 2
     part_out[...] = jnp.concatenate([part[:fold, :], part[fold:, :]], axis=1)
 
-    @pl.loop(1, planes)
-    def _(i):
-        remote(part_out, part_in.at[z], one_sent, one_recv, me, ring(z + i, planes)).start()
+    @pl.loop(0, planes - 1)
+    def _(n):
+        plane = ring(z + far_first(n, half), planes)
+        remote(part_out, part_in.at[z], one_sent, one_recv, me, plane).start()
 
     part_in[z] = part_out[...]
     spread_out(spot_copy, spot_twin)
-    hand_on(spot_copy, spot_twin)
-
-    @pl.when(takes_strips)
-    def _():
-        @pl.loop(0, chips)
-        def _(chip):
-            landed = strip_rows(mixed, chip)
-            settle(landed, mixed_recv.at[chip])
-            remote(landed, landed, mixed_twin_sent, mixed_twin_recv, twin, z).start()
 
     def send_hidden(j):
         for cr in range(2):
@@ -279,6 +276,14 @@
     def _(j):
         send_hidden(j)
 
+    @pl.when(takes_strips)
+    def _():
+        @pl.loop(0, chips)
+        def _(chip):
+            landed = strip_rows(mixed, chip)
+            settle(landed, mixed_recv.at[chip])
+            remote(landed, landed, mixed_twin_sent, mixed_twin_recv, twin, z).start()
+
     settle(part_in.at[pl.ds(0, planes - 1)], one_recv)
     summed = part_in[0]
     for b in range(1, planes):
@@ -286,6 +291,7 @@
     part_sum[core] = summed
     swap = remote(part_sum.at[core], part_sum.at[core], two_sent, two_recv, twin, z)
     swap.start()
+    hand_on(spot_copy, spot_twin)
     swap.wait_recv()
 
     factor = scale[0] / (vocab_local * planes)
@@ -374,26 +380,24 @@
             pl.ds(pl.multiple_of(plane * strip, strip), strip), u * span : (u + 1) * span
         ]
 
-    def place(way, step, u):
-        return (way * half + step) * UNITS + u
-
-    def ring_copy(way, step, u):
-        index = place(way, step, u)
-        neighbour = ring(z + 1 - 2 * way, planes)
-        return remote(
-            stage.at[index], inbox.at[index], ring_sent, ring_recv.at[index], me, neighbour
-        )
-
-    def owner_of(way, step):
-        return ring(z + (1 - 2 * way) * (half - step), planes)
-
-    def ring_step(step, way, u, follows):
-        value = own_part(owner_of(way, step), u)
-        if follows:
-            ring_copy(way, step - 1, u).wait_recv()
-            value = value + inbox[place(way, step - 1, u)].astype(F32)
-        stage[place(way, step, u)] = value.astype(BF16)
-        ring_copy(way, step, u).start()
+    def place(way, u, slot):
+        return (way * UNITS + u) * SLOTS + slot
+
+    def own(way, distance, u):
+        return own_part(ring(z + (1 - 2 * way) * distance, planes), u)
+
+    def send(way, u, slot, hops, value):
+        index = place(way, u, slot)
+        stage[index] = value.astype(BF16)
+        target = ring(z + (1 - 2 * way) * hops, planes)
+        remote(
+            stage.at[index], inbox.at[index], ring_sent, ring_recv.at[index], me, target
+        ).start()
+
+    def take(way, u, slot):
+        index = place(way, u, slot)
+        settle(inbox.at[index], ring_recv.at[index])
+        return inbox[index].astype(F32)
 
     def add_weight(m):
         chip = ring(column + m, chips)
@@ -407,36 +411,49 @@
             preferred_element_type=F32,
         )
 
+    def begins(way, u):
+        return half if (u < UNITS // 2) == (way == 0) else half - 1
+
     for u in range(UNITS):
-        way = 0 if u < UNITS // 2 else 1
         sum_unit(u)
-        ring_step(0, way, u, False)
-        ring_step(1, 1 - way, u, False)
+        for way in (0, 1) if u < UNITS // 2 else (1, 0):
+            far = begins(way, u)
+            send(way, u, 0, 2, own(way, far, u))
+            send(way, u, 1, 1, own(way, far - 1, u))
+            if far == half:
+                send(way, u, 2, 1, own(way, far - 3, u))
     for u in range(UNITS):
-        ring_step(1, 0 if u < UNITS // 2 else 1, u, True)
+        for way in (0, 1) if u < UNITS // 2 else (1, 0):
+            far = begins(way, u) - 2
+            value = own(way, far, u) + take(way, u, 0) + take(way, u, 1)
+            send(way, u, 3, far - half + 4, value)
 
     @pl.loop(chips // 2, chips)
     def _(j):
         send_hidden(j)
 
     total[...] = jnp.zeros_like(total)
-
-    @pl.loop(2, half)
-    def _(step):
+    weighed = 0
+    for slot in range(4, SLOTS):
+        distance = half - slot
         for u in range(UNITS):
-            for way in range(2):
-                ring_step(step, way, u, True)
-
-        @pl.when(step >= 3)
-        def _():
-            for i in range(2):
-                add_weight(2 * (step - 3) + i)
+            for way in (0, 1) if u < UNITS // 2 else (1, 0):
+                value = own(way, distance, u) + take(way, u, slot - 1)
+                if slot == 4 and begins(way, u) == half:
+                    value = value + take(way, u, 2)
+                send(way, u, slot, 1, value)
+        if slot > 4:
+
+            @pl.loop(weighed, weighed + 3)
+            def _(m):
+                add_weight(m)
+
+            weighed += 3
 
     for u in range(UNITS):
         value = own_part(z, u)
         for way in range(2):
-            ring_copy(way, half - 1, u).wait_recv()
-            value = value + inbox[place(way, half - 1, u)].astype(F32)
+            value = value + take(way, u, SLOTS - 1)
         last[:, u * span : (u + 1) * span] = value.astype(BF16)
 
         @pl.loop(u * (chips // UNITS), (u + 1) * (chips // UNITS))
@@ -452,7 +469,7 @@
             def _():
                 pltpu.make_async_copy(block, dest, last_recv).start()
 
-    @pl.loop(max(0, 2 * (half - 3)), chips)
+    @pl.loop(weighed, chips)
     def _(m):
         add_weight(m)
 
@@ -522,7 +539,7 @@
     sequences = 4 * groups
     vmem = pl.BlockSpec(memory_space=pltpu.VMEM)
     main = pl.BlockSpec(memory_space=pltpu.HBM)
-    units = 2 * half * UNITS
+    units = 2 * UNITS * SLOTS
     span = rows * chips // UNITS
     dma = pltpu.SemaphoreType.DMA
     grad_query, grad_passage, grad_weight = pl.pallas_call(

time: 79.6 us -> 93.3 us (1.17)
  the two profiles are of different devices: /device:TPU:6 before, /device:TPU:5 now
where the time goes in v5:
time: 93.3 us; the launch traced here: 93.1 us
  Pallas kernels  91.8 us (98%)
  between operations  1.29 us (1%)
    pallas_call x1, Pallas kernels, on_device(): pl.pallas_call(functools.partial(kernel, groups, planes), out_shape=(jax....  89.9 us
    pallas_call x1, Pallas kernels, on_device(): pl.pallas_call(hand_over, out_shape=tuple((jax.ShapeDtypeStruct(r.shape,...  1.93 us

profile of v5, /device:TPU:5, one launch (start us, length us, event | category | flops | bytes accessed | tf_op | source)
XLA Modules:
  0.0 93.1 jit_solution(8636103287618198559)
XLA Ops:
  1.3 89.9 %shard_map.112 = (bf16[64,256]{1,0:T(8,128)(2,1)}, bf16[192,256]{1,0:T(8,128)(2,1)}, f32[1024,128]{1,0:T(8,128)}) custom-call(bf16[64,4096]{1,0:T(8,128)(2,1)} %bitcast.6, bf16[192,4096]{1,0:T(8,128)(2,1)} %bitcast.5, f32[2,32,1024]{2,1,0:T(8,128)} %query_logits_in.1, f32[2,96,1024]{2,1,0:T(8,128)} %passage_logits_in.1, bf16[1024,128]{1,0:T(8,128)(2,1)} %weight_in.1, ...), custom_call_target="tpu_custom_call" | custom-call | tf_op jit(solution)/shard_map/pallas_call | solution.py:545
  91.2 1.9 %shard_map.113 = (bf16[64,256]{1,0:T(8,128)(2,1)}, bf16[192,256]{1,0:T(8,128)(2,1)}, f32[1024,128]{1,0:T(8,128)}) custom-call(bf16[64,256]{1,0:T(8,128)(2,1)} %get-tuple-element.9.refs_0_, bf16[192,256]{1,0:T(8,128)(2,1)} %get-tuple-element.10.refs_1_, f32[1024,128]{1,0:T(8,128)} %get-tuple-element.11.refs_2_), custom_call_target="tpu_custom_call" | custom-call | tf_op jit(solution)/shard_map/pallas_call | solution.py:607

commit v6 on v4

--- a/solution.py
+++ b/solution.py
@@ -63,6 +63,9 @@
     last,
     final,
     total,
+    query_out,
+    passage_out,
+    weight_out,
     load,
     sent,
     pool_recv,
@@ -76,6 +79,7 @@
     hidden_recv,
     ring_recv,
     last_recv,
+    leave,
 ):
     chips = groups // 2
     half = planes // 2
@@ -343,8 +347,8 @@
     def _():
         settle(mixed, mixed_twin_recv)
 
-    def build(group):
-        start = 0
+    def table_of(group):
+        parts = []
         for k in range(4):
             length = query_length if k < 2 else passage_length
             push_row = push[pl.ds(k * groups + group, 1), :]
@@ -352,22 +356,23 @@
                 [spots[group, k : k + 1, :], spots[group, 4 + k : 5 + k, :]], axis=1
             )
             positions = lax.broadcasted_iota(jnp.int32, (length, vocab_local), 0).astype(F32)
-            tables[pl.ds(pl.multiple_of(group * rows + start, 32), length), :] = jnp.where(
-                positions == spot_row, push_row, 0.0
-            ).astype(BF16)
-            start += length
+            parts.append(jnp.where(positions == spot_row, push_row, 0.0).astype(BF16))
+        return jnp.concatenate(parts, axis=0)
+
+    def keep(group, value):
+        tables[pl.ds(pl.multiple_of(group * rows, rows), rows), :] = value
 
     def sum_unit(u):
-        @pl.loop(u * (chips // UNITS), (u + 1) * (chips // UNITS))
-        def _(j):
-            group = 2 * j + core
-            build(group)
-            partial[:, pl.ds(pl.multiple_of(j * rows, rows), rows)] = lax.dot_general(
-                mixed[...],
-                tables[pl.ds(pl.multiple_of(group * rows, rows), rows), :],
-                (((1,), (1,)), ((), ())),
-                preferred_element_type=F32,
-            )
+        members = [2 * j + core for j in range(u * (chips // UNITS), (u + 1) * (chips // UNITS))]
+        parts = [table_of(group) for group in members]
+        partial[:, u * span : (u + 1) * span] = lax.dot_general(
+            mixed[...],
+            jnp.concatenate(parts, axis=0),
+            (((1,), (1,)), ((), ())),
+            preferred_element_type=F32,
+        )
+        for group, value in zip(members, parts):
+            keep(group, value)
 
     def own_part(plane, u):
         return partial[
@@ -397,7 +402,8 @@
 
     def add_weight(m):
         chip = ring(column + m, chips)
-        build(2 * chip + 1 - core)
+        other = 2 * chip + 1 - core
+        keep(other, table_of(other))
         first = pl.multiple_of(chip * 2 * rows, 64)
         settle(hidden.at[pl.ds(first, 2 * rows)], hidden_recv.at[chip])
         total[...] += lax.dot_general(
@@ -456,12 +462,21 @@
     def _(m):
         add_weight(m)
 
-    grad_weight[...] = total[...].T
+    results = [
+        pltpu.make_async_copy(source, dest, leave.at[n])
+        for n, (source, dest) in enumerate(
+            ((weight_out, grad_weight), (query_out, grad_query), (passage_out, grad_passage))
+        )
+    ]
+    weight_out[...] = total[...].T
+    results[0].start()
 
     settle(final, last_recv)
     whole = final[...].astype(F32).T.astype(BF16)
-    grad_query[...] = whole[:query_rows, :]
-    grad_passage[...] = whole[query_rows:, :]
+    query_out[...] = whole[:query_rows, :]
+    passage_out[...] = whole[query_rows:, :]
+    for copy in results[1:]:
+        copy.start()
 
     settle(pools.at[pl.ds(0, chips - 1)], pool_sent)
     settle(pools.at[pl.ds(0, chips)], twin_sent)
@@ -482,6 +497,8 @@
     settle(hidden.at[pl.ds(0, (groups - 1) * rows)], hidden_sent)
     settle(stage.at[pl.ds(0, (2 * half - 1) * UNITS)], ring_sent)
     settle(last.at[:, pl.ds(0, (chips - 1) * rows)], last_sent)
+    for copy in results:
+        copy.wait()
 
 
 def hand_over(*refs):
@@ -520,7 +537,6 @@
     half = planes // 2
     strip = 2 * block // chips
     sequences = 4 * groups
-    vmem = pl.BlockSpec(memory_space=pltpu.VMEM)
     main = pl.BlockSpec(memory_space=pltpu.HBM)
     units = 2 * half * UNITS
     span = rows * chips // UNITS
@@ -533,7 +549,7 @@
             jax.ShapeDtypeStruct((vocab_local, block), F32),
         ),
         in_specs=[main] * 8 + [pl.BlockSpec(memory_space=pltpu.SMEM)],
-        out_specs=(vmem, vmem, vmem),
+        out_specs=(main,) * 3,
         scratch_shapes=[
             pltpu.VMEM(query_logits.shape, F32),
             pltpu.VMEM(passage_logits.shape, F32),
@@ -558,6 +574,9 @@
             pltpu.VMEM((strip, chips * rows), BF16),
             pltpu.VMEM((2 * block, rows), BF16),
             pltpu.VMEM((block, vocab_local), F32),
+            pltpu.VMEM((query_rows, 2 * block), BF16),
+            pltpu.VMEM((passage_rows, 2 * block), BF16),
+            pltpu.VMEM((vocab_local, block), F32),
             dma((6,)),
             dma((11,)),
             dma((chips,)),
@@ -571,6 +590,7 @@
             dma((chips,)),
             dma((units,)),
             dma,
+            dma((3,)),
         ],
         compiler_params=pltpu.CompilerParams(
             collective_id=0, has_side_effects=True, vmem_limit_bytes=60 * 1024 * 1024

time: 79.6 us -> 80.5 us (1.011); the launches traced: 79.5 us -> 79.3 us
  no operation moved by 1% of the time
where the time goes in v6:
time: 80.5 us; the launch traced here: 79.3 us
  Pallas kernels  78.1 us (97%)
  between operations  1.29 us (2%)
    pallas_call x1, Pallas kernels, on_device(): pl.pallas_call(functools.partial(kernel, groups, planes), out_shape=(jax....  76.1 us
    pallas_call x1, Pallas kernels, on_device(): pl.pallas_call(hand_over, out_shape=tuple((jax.ShapeDtypeStruct(r.shape,...  1.93 us

profile of v6, /device:TPU:6, one launch (start us, length us, event | category | flops | bytes accessed | tf_op | source)
XLA Modules:
  0.0 79.3 jit_solution(1888776876110175577)
XLA Ops:
  1.3 76.1 %shard_map.112 = (bf16[64,256]{1,0:T(8,128)(2,1)}, bf16[192,256]{1,0:T(8,128)(2,1)}, f32[1024,128]{1,0:T(8,128)}) custom-call(bf16[64,4096]{1,0:T(8,128)(2,1)} %bitcast.6, bf16[192,4096]{1,0:T(8,128)(2,1)} %bitcast.5, f32[2,32,1024]{2,1,0:T(8,128)} %query_logits_in.1, f32[2,96,1024]{2,1,0:T(8,128)} %passage_logits_in.1, bf16[1024,128]{1,0:T(8,128)(2,1)} %weight_in.1, ...), custom_call_target="tpu_custom_call" | custom-call | tf_op jit(solution)/shard_map/pallas_call | solution.py:544
  77.4 1.9 %shard_map.113 = (bf16[64,256]{1,0:T(8,128)(2,1)}, bf16[192,256]{1,0:T(8,128)(2,1)}, f32[1024,128]{1,0:T(8,128)}) custom-call(bf16[64,256]{1,0:T(8,128)(2,1)} %get-tuple-element.9.refs_0_, bf16[192,256]{1,0:T(8,128)(2,1)} %get-tuple-element.10.refs_1_, f32[1024,128]{1,0:T(8,128)} %get-tuple-element.11.refs_2_), custom_call_target="tpu_custom_call" | custom-call | tf_op jit(solution)/shard_map/pallas_call | solution.py:610

commit v7 on v6

--- a/solution.py
+++ b/solution.py
@@ -55,6 +55,7 @@
     part_sum,
     turned,
     mixed,
+    held,
     hidden,
     tables,
     partial,
@@ -127,6 +128,8 @@
                 (passage_logits_in, passage_logits),
                 (weight_in, weight),
                 (positive_in, positive),
+                (query_hidden, held.at[pl.ds(0, query_rows)]),
+                (passage_hidden, held.at[pl.ds(query_rows, rows - query_rows)]),
             )
         )
     ]
@@ -259,29 +262,27 @@
             settle(landed, mixed_recv.at[chip])
             remote(landed, landed, mixed_twin_sent, mixed_twin_recv, twin, z).start()
 
-    def send_hidden(j):
-        for cr in range(2):
-            target = 2 * ring(column - j, chips) + cr
-            columns = pl.ds(pl.multiple_of(target * width, width), width)
-            for source, start, count in (
-                (query_hidden, 0, query_rows),
-                (passage_hidden, query_rows, rows - query_rows),
-            ):
-                block = source.at[:, columns]
-                dest = hidden.at[pl.ds(pl.multiple_of(me * rows + start, 64), count)]
-                arrived = hidden_recv.at[column]
-
-                @pl.when(target != me)
-                def _():
-                    remote(block, dest, hidden_sent, arrived, target, z).start()
-
-                @pl.when(target == me)
-                def _():
-                    pltpu.make_async_copy(block, dest, arrived).start()
-
-    @pl.loop(0, chips // 2)
-    def _(j):
-        send_hidden(j)
+    pairs = chips // 2
+    pair = lax.div(column, 2)
+
+    def send_hidden(i):
+        dest = hidden.at[pl.ds(pl.multiple_of(me * rows, rows), rows)]
+        arrived = hidden_recv.at[pair]
+        for n in range(4):
+            target = 4 * ring(pair - i, pairs) + n
+            block = held.at[:, pl.ds(pl.multiple_of(target * width, width), width)]
+
+            @pl.when(target != me)
+            def _():
+                remote(block, dest, hidden_sent, arrived, target, z).start()
+
+            @pl.when(target == me)
+            def _():
+                pltpu.make_async_copy(block, dest, arrived).start()
+
+    @pl.loop(0, pairs // 2)
+    def _(i):
+        send_hidden(i)
 
     settle(part_in.at[pl.ds(0, planes - 1)], one_recv)
     summed = part_in[0]
@@ -400,15 +401,16 @@
         stage[place(way, step, u)] = value.astype(BF16)
         ring_copy(way, step, u).start()
 
-    def add_weight(m):
-        chip = ring(column + m, chips)
-        other = 2 * chip + 1 - core
-        keep(other, table_of(other))
-        first = pl.multiple_of(chip * 2 * rows, 64)
-        settle(hidden.at[pl.ds(first, 2 * rows)], hidden_recv.at[chip])
+    def add_weight(i):
+        taken = ring(pair + i, pairs)
+        for n in range(2):
+            other = 2 * (2 * taken + n) + 1 - core
+            keep(other, table_of(other))
+        batch = pl.ds(pl.multiple_of(taken * 4 * rows, rows), 4 * rows)
+        settle(hidden.at[batch], hidden_recv.at[taken])
         total[...] += lax.dot_general(
-            hidden[pl.ds(first, 2 * rows), :],
-            tables[pl.ds(first, 2 * rows), :],
+            hidden[batch, :],
+            tables[batch, :],
             (((0,), (0,)), ((), ())),
             preferred_element_type=F32,
         )
@@ -421,9 +423,9 @@
     for u in range(UNITS):
         ring_step(1, 0 if u < UNITS // 2 else 1, u, True)
 
-    @pl.loop(chips // 2, chips)
-    def _(j):
-        send_hidden(j)
+    @pl.loop(pairs // 2, pairs)
+    def _(i):
+        send_hidden(i)
 
     total[...] = jnp.zeros_like(total)
 
@@ -432,11 +434,11 @@
         for u in range(UNITS):
             for way in range(2):
                 ring_step(step, way, u, True)
-
-        @pl.when(step >= 3)
-        def _():
-            for i in range(2):
-                add_weight(2 * (step - 3) + i)
+            if u == UNITS // 2 - 1:
+
+                @pl.when(step >= 3)
+                def _():
+                    add_weight(step - 3)
 
     for u in range(UNITS):
         value = own_part(z, u)
@@ -458,9 +460,9 @@
             def _():
                 pltpu.make_async_copy(block, dest, last_recv).start()
 
-    @pl.loop(max(0, 2 * (half - 3)), chips)
-    def _(m):
-        add_weight(m)
+    @pl.loop(max(0, half - 3), pairs)
+    def _(i):
+        add_weight(i)
 
     results = [
         pltpu.make_async_copy(source, dest, leave.at[n])
@@ -566,6 +568,7 @@
             pltpu.VMEM((2, chips, sequences), F32),
             pltpu.VMEM((block, vocab_local), BF16),
             pltpu.VMEM((2 * block, vocab_local), BF16),
+            pltpu.VMEM((rows, width), BF16),
             pltpu.VMEM((groups * rows, block), BF16),
             pltpu.VMEM((groups * rows, vocab_local), BF16),
             pltpu.VMEM((2 * block, chips * rows), F32),
@@ -577,7 +580,7 @@
             pltpu.VMEM((query_rows, 2 * block), BF16),
             pltpu.VMEM((passage_rows, 2 * block), BF16),
             pltpu.VMEM((vocab_local, block), F32),
-            dma((6,)),
+            dma((8,)),
             dma((11,)),
             dma((chips,)),
             dma,
@@ -587,7 +590,7 @@
             dma,
             dma((chips,)),
             dma,
-            dma((chips,)),
+            dma((chips // 2,)),
             dma((units,)),
             dma,
             dma((3,)),

time: 80.5 us -> 81.8 us (1.016); the launches traced: 79.3 us -> 81.7 us
  Pallas kernels: 78.1 us -> 80.4 us
    pallas_call x1, Pallas kernels: 76.1 us -> 78.5 us  [on_device(): pl.pallas_call(functools.partial(kernel, groups, planes), out_shape=(jax....]
where the time goes in v7:
time: 81.8 us; the launch traced here: 81.7 us
  Pallas kernels  80.4 us (98%)
  between operations  1.29 us (2%)
    pallas_call x1, Pallas kernels, on_device(): pl.pallas_call(functools.partial(kernel, groups, planes), out_shape=(jax....  78.5 us
    pallas_call x1, Pallas kernels, on_device(): pl.pallas_call(hand_over, out_shape=tuple((jax.ShapeDtypeStruct(r.shape,...  1.93 us

profile of v7, /device:TPU:6, one launch (start us, length us, event | category | flops | bytes accessed | tf_op | source)
XLA Modules:
  0.0 81.7 jit_solution(5056377969464739667)
XLA Ops:
  1.3 78.5 %shard_map.112 = (bf16[64,256]{1,0:T(8,128)(2,1)}, bf16[192,256]{1,0:T(8,128)(2,1)}, f32[1024,128]{1,0:T(8,128)}) custom-call(bf16[64,4096]{1,0:T(8,128)(2,1)} %bitcast.6, bf16[192,4096]{1,0:T(8,128)(2,1)} %bitcast.5, f32[2,32,1024]{2,1,0:T(8,128)} %query_logits_in.1, f32[2,96,1024]{2,1,0:T(8,128)} %passage_logits_in.1, bf16[1024,128]{1,0:T(8,128)(2,1)} %weight_in.1, ...), custom_call_target="tpu_custom_call" | custom-call | tf_op jit(solution)/shard_map/pallas_call | solution.py:546
  79.8 1.9 %shard_map.113 = (bf16[64,256]{1,0:T(8,128)(2,1)}, bf16[192,256]{1,0:T(8,128)(2,1)}, f32[1024,128]{1,0:T(8,128)}) custom-call(bf16[64,256]{1,0:T(8,128)(2,1)} %get-tuple-element.9.refs_0_, bf16[192,256]{1,0:T(8,128)(2,1)} %get-tuple-element.10.refs_1_, f32[1024,128]{1,0:T(8,128)} %get-tuple-element.11.refs_2_), custom_call_target="tpu_custom_call" | custom-call | tf_op jit(solution)/shard_map/pallas_call | solution.py:613

commit v8 on v7

--- a/solution.py
+++ b/solution.py
@@ -165,42 +165,31 @@
             [line[:, :middle] for line in lines] + [line[:, middle:] for line in lines], axis=0
         )
 
-    pools[me] = folded([f[0] for f in found])
-    spots[me] = folded([f[1] for f in found])
+    def slot_of(group):
+        return lax.rem(group, 2) * chips + lax.div(group, 2)
+
+    mine = slot_of(me)
+    pools[mine] = folded([f[0] for f in found])
+    spots[mine] = folded([f[1] for f in found])
     for copy in loads[4:]:
         copy.wait()
     turned[...] = weight[...].astype(F32).T.astype(BF16)
 
     pl.semaphore_wait(barrier, groups + planes - 2)
 
-    def pool_copy(group, target, m):
-        return remote(pools.at[group], pools.at[group], pool_sent, pool_recv.at[m], target, z)
-
-    def pool_twin(group):
-        return remote(pools.at[group], pools.at[group], twin_sent, twin_recv, twin, z)
-
-    def spot_copy(group, target, m):
-        return remote(spots.at[group], spots.at[group], spot_sent, spot_recv.at[m], target, z)
-
-    def spot_twin(group):
-        return remote(spots.at[group], spots.at[group], spot_twin_sent, spot_twin_recv, twin, z)
-
-    def spread_out(copy, twin_copy):
+    def spread_out(ref, send, recv):
         @pl.loop(1, chips)
         def _(m):
-            copy(me, 2 * ring(column + m, chips) + core, m).start()
-
-        twin_copy(me).start()
-
-    def hand_on(copy, twin_copy):
-        @pl.loop(1, chips)
-        def _(m):
-            group = 2 * ring(column - m, chips) + core
-            copy(group, me, m).wait_recv()
-            twin_copy(group).start()
-
-    spread_out(pool_copy, pool_twin)
-    hand_on(pool_copy, pool_twin)
+            target = 2 * ring(column + m, chips) + core
+            remote(ref.at[mine], ref.at[mine], send, recv, target, z).start()
+
+    def pass_on(ref, recv, twin_send, twin_arrived):
+        settle(ref.at[pl.ds(0, chips - 1)], recv)
+        blocks = ref.at[pl.ds(core * chips, chips)]
+        remote(blocks, blocks, twin_send, twin_arrived, twin, z).start()
+
+    spread_out(pools, pool_sent, pool_recv)
+    pass_on(pools, pool_recv, twin_sent, twin_recv)
 
     def strip_rows(ref, index):
         return ref.at[pl.ds(pl.multiple_of(index * strip, strip), strip)]
@@ -215,7 +204,7 @@
                 strip_rows(turned, chip - core * half),
                 strip_rows(mixed, column),
                 mixed_sent,
-                mixed_recv.at[column],
+                mixed_recv,
                 2 * chip + core,
                 z,
             ).start()
@@ -225,7 +214,7 @@
             pltpu.make_async_copy(
                 strip_rows(turned, chip - core * half),
                 strip_rows(mixed, column),
-                mixed_recv.at[column],
+                mixed_recv,
             ).start()
 
     takes_strips = core == lax.div(column, half)
@@ -251,16 +240,13 @@
         remote(part_out, part_in.at[z], one_sent, one_recv, me, ring(z + i, planes)).start()
 
     part_in[z] = part_out[...]
-    spread_out(spot_copy, spot_twin)
-    hand_on(spot_copy, spot_twin)
+    spread_out(spots, spot_sent, spot_recv)
+    pass_on(spots, spot_recv, spot_twin_sent, spot_twin_recv)
 
     @pl.when(takes_strips)
     def _():
-        @pl.loop(0, chips)
-        def _(chip):
-            landed = strip_rows(mixed, chip)
-            settle(landed, mixed_recv.at[chip])
-            remote(landed, landed, mixed_twin_sent, mixed_twin_recv, twin, z).start()
+        settle(mixed, mixed_recv)
+        remote(mixed, mixed, mixed_twin_sent, mixed_twin_recv, twin, z).start()
 
     pairs = chips // 2
     pair = lax.div(column, 2)
@@ -305,7 +291,9 @@
     lane = lax.broadcasted_iota(jnp.int32, scores.shape, 1)
 
     def natural(index):
-        return jnp.where(index < groups, 2 * index, 2 * (index - groups) + 1)
+        k = jnp.where(index < groups, 0, 1)
+        held_at = index - groups * k
+        return 2 * jnp.where(held_at < chips, 2 * held_at, 2 * (held_at - chips) + 1) + k
 
     wanted = jnp.sum(
         jnp.where(
@@ -350,11 +338,12 @@
 
     def table_of(group):
         parts = []
+        slot = slot_of(group)
         for k in range(4):
             length = query_length if k < 2 else passage_length
-            push_row = push[pl.ds(k * groups + group, 1), :]
+            push_row = push[pl.ds(k * groups + slot, 1), :]
             spot_row = jnp.concatenate(
-                [spots[group, k : k + 1, :], spots[group, 4 + k : 5 + k, :]], axis=1
+                [spots[slot, k : k + 1, :], spots[slot, 4 + k : 5 + k, :]], axis=1
             )
             positions = lax.broadcasted_iota(jnp.int32, (length, vocab_local), 0).astype(F32)
             parts.append(jnp.where(positions == spot_row, push_row, 0.0).astype(BF16))
@@ -582,13 +571,13 @@
             pltpu.VMEM((vocab_local, block), F32),
             dma((8,)),
             dma((11,)),
-            dma((chips,)),
-            dma,
-            dma((chips,)),
-            dma,
-            dma,
-            dma,
-            dma((chips,)),
+            dma,
+            dma,
+            dma,
+            dma,
+            dma,
+            dma,
+            dma,
             dma,
             dma((chips // 2,)),
             dma((units,)),

time: 81.8 us -> 81.8 us (level)
  no operation moved by 1% of the time
where the time goes in v8:
time: 81.8 us; the launch traced here: 81.6 us
  Pallas kernels  80.3 us (98%)
  between operations  1.29 us (2%)
    pallas_call x1, Pallas kernels, on_device(): pl.pallas_call(functools.partial(kernel, groups, planes), out_shape=(jax....  78.3 us
    pallas_call x1, Pallas kernels, on_device(): pl.pallas_call(hand_over, out_shape=tuple((jax.ShapeDtypeStruct(r.shape,...  1.93 us

profile of v8, /device:TPU:6, one launch (start us, length us, event | category | flops | bytes accessed | tf_op | source)
XLA Modules:
  0.0 81.6 jit_solution(18167891079465802608)
XLA Ops:
  1.3 78.3 %shard_map.112 = (bf16[64,256]{1,0:T(8,128)(2,1)}, bf16[192,256]{1,0:T(8,128)(2,1)}, f32[1024,128]{1,0:T(8,128)}) custom-call(bf16[64,4096]{1,0:T(8,128)(2,1)} %bitcast.6, bf16[192,4096]{1,0:T(8,128)(2,1)} %bitcast.5, f32[2,32,1024]{2,1,0:T(8,128)} %query_logits_in.1, f32[2,96,1024]{2,1,0:T(8,128)} %passage_logits_in.1, bf16[1024,128]{1,0:T(8,128)(2,1)} %weight_in.1, ...), custom_call_target="tpu_custom_call" | custom-call | tf_op jit(solution)/shard_map/pallas_call | solution.py:535
  79.6 1.9 %shard_map.113 = (bf16[64,256]{1,0:T(8,128)(2,1)}, bf16[192,256]{1,0:T(8,128)(2,1)}, f32[1024,128]{1,0:T(8,128)}) custom-call(bf16[64,256]{1,0:T(8,128)(2,1)} %get-tuple-element.9.refs_0_, bf16[192,256]{1,0:T(8,128)(2,1)} %get-tuple-element.10.refs_1_, f32[1024,128]{1,0:T(8,128)} %get-tuple-element.11.refs_2_), custom_call_target="tpu_custom_call" | custom-call | tf_op jit(solution)/shard_map/pallas_call | solution.py:602

commit v9 on v8

--- a/solution.py
+++ b/solution.py
@@ -55,7 +55,6 @@
     part_sum,
     turned,
     mixed,
-    held,
     hidden,
     tables,
     partial,
@@ -128,8 +127,6 @@
                 (passage_logits_in, passage_logits),
                 (weight_in, weight),
                 (positive_in, positive),
-                (query_hidden, held.at[pl.ds(0, query_rows)]),
-                (passage_hidden, held.at[pl.ds(query_rows, rows - query_rows)]),
             )
         )
     ]
@@ -252,19 +249,24 @@
     pair = lax.div(column, 2)
 
     def send_hidden(i):
-        dest = hidden.at[pl.ds(pl.multiple_of(me * rows, rows), rows)]
         arrived = hidden_recv.at[pair]
         for n in range(4):
             target = 4 * ring(pair - i, pairs) + n
-            block = held.at[:, pl.ds(pl.multiple_of(target * width, width), width)]
-
-            @pl.when(target != me)
-            def _():
-                remote(block, dest, hidden_sent, arrived, target, z).start()
-
-            @pl.when(target == me)
-            def _():
-                pltpu.make_async_copy(block, dest, arrived).start()
+            columns = pl.ds(pl.multiple_of(target * width, width), width)
+            for source, start, count in (
+                (query_hidden, 0, query_rows),
+                (passage_hidden, query_rows, rows - query_rows),
+            ):
+                block = source.at[:, columns]
+                dest = hidden.at[pl.ds(pl.multiple_of(me * rows + start, 64), count)]
+
+                @pl.when(target != me)
+                def _():
+                    remote(block, dest, hidden_sent, arrived, target, z).start()
+
+                @pl.when(target == me)
+                def _():
+                    pltpu.make_async_copy(block, dest, arrived).start()
 
     @pl.loop(0, pairs // 2)
     def _(i):
@@ -557,7 +559,6 @@
             pltpu.VMEM((2, chips, sequences), F32),
             pltpu.VMEM((block, vocab_local), BF16),
             pltpu.VMEM((2 * block, vocab_local), BF16),
-            pltpu.VMEM((rows, width), BF16),
             pltpu.VMEM((groups * rows, block), BF16),
             pltpu.VMEM((groups * rows, vocab_local), BF16),
             pltpu.VMEM((2 * block, chips * rows), F32),
@@ -569,7 +570,7 @@
             pltpu.VMEM((query_rows, 2 * block), BF16),
             pltpu.VMEM((passage_rows, 2 * block), BF16),
             pltpu.VMEM((vocab_local, block), F32),
-            dma((8,)),
+            dma((6,)),
             dma((11,)),
             dma,
             dma,

time: 81.8 us -> 82.3 us (level)
  no operation moved by 1% of the time
where the time goes in v9:
time: 82.3 us; the launch traced here: 82.1 us
  Pallas kernels  80.8 us (98%)
  between operations  1.29 us (2%)
    pallas_call x1, Pallas kernels, on_device(): pl.pallas_call(functools.partial(kernel, groups, planes), out_shape=(jax....  78.9 us
    pallas_call x1, Pallas kernels, on_device(): pl.pallas_call(hand_over, out_shape=tuple((jax.ShapeDtypeStruct(r.shape,...  1.93 us

profile of v9, /device:TPU:6, one launch (start us, length us, event | category | flops | bytes accessed | tf_op | source)
XLA Modules:
  0.0 82.1 jit_solution(18096988687883986974)
XLA Ops:
  1.3 78.9 %shard_map.112 = (bf16[64,256]{1,0:T(8,128)(2,1)}, bf16[192,256]{1,0:T(8,128)(2,1)}, f32[1024,128]{1,0:T(8,128)}) custom-call(bf16[64,4096]{1,0:T(8,128)(2,1)} %bitcast.6, bf16[192,4096]{1,0:T(8,128)(2,1)} %bitcast.5, f32[2,32,1024]{2,1,0:T(8,128)} %query_logits_in.1, f32[2,96,1024]{2,1,0:T(8,128)} %passage_logits_in.1, bf16[1024,128]{1,0:T(8,128)(2,1)} %weight_in.1, ...), custom_call_target="tpu_custom_call" | custom-call | tf_op jit(solution)/shard_map/pallas_call | solution.py:537
  80.2 1.9 %shard_map.113 = (bf16[64,256]{1,0:T(8,128)(2,1)}, bf16[192,256]{1,0:T(8,128)(2,1)}, f32[1024,128]{1,0:T(8,128)}) custom-call(bf16[64,256]{1,0:T(8,128)(2,1)} %get-tuple-element.9.refs_0_, bf16[192,256]{1,0:T(8,128)(2,1)} %get-tuple-element.10.refs_1_, f32[1024,128]{1,0:T(8,128)} %get-tuple-element.11.refs_2_), custom_call_target="tpu_custom_call" | custom-call | tf_op jit(solution)/shard_map/pallas_call | solution.py:603
